TPU v7x, 128 devices: a whole 4x4x4 slice. The times are simulated.
128 devices in a mesh: tb: 16 (over z_hi, y, core), ti: 8 (over z_lo, x).
Axes of the slice: x: 4, y: 4, z: 4 (z_hi: 2, z_lo: 2; z = z_hi * 2 + z_lo), core: 2. Of those that a mesh axis runs over, the one named last changes fastest.
Arguments:
- sources: float32 [256, 256, 512], P(('tb', 'ti')), may hold values from -4 to 4
- initial_state: float32 [256, 512], replicated, may hold values from -6 to 6
- roughness: float32 [256, 512], replicated, may hold values from 0.5 to 1
- region_ids: int32 [16, 16], replicated, may hold values from 0 to 15
- diffusion_table: float32 [16], replicated, may hold values from 0.02 to 0.1
- velocity_table: float32 [16, 2], replicated, may hold values from -0.05 to 0.05
Outputs:
- iterate: float32 [256, 256, 512], P(('tb', 'ti'))
All inputs are finite; a program needn't handle non-finite values.
Results may differ from a plain program's by a relative error of at most 0.00002.
Values sent between devices are 32-bit elements; how exact they have to be, the bound alone decides.
A program may use at most 128 MiB of HBM per device.

v0:
```python
import jax
import jax.numpy as jnp
from jax import lax
from jax.sharding import PartitionSpec as P


def passed_along(value, axis, steps):
    count = lax.axis_size(axis)
    initial, last = (max(0, -steps), min(count, count - steps))
    return lax.ppermute(value, axis, [(source, source + steps) for source in range(initial, last)])


def coefficients(region_ids, diffusion_table, velocity_table, roughness):
    width_x = roughness.shape[0] // region_ids.shape[0]
    width_y = roughness.shape[1] // region_ids.shape[1]
    entries = jnp.arange(diffusion_table.shape[0], dtype=jnp.int32)
    onehot = (region_ids[:, :, None] == entries[None, None, :]).astype(jnp.float32)
    diffusion_blocks = jnp.sum(onehot * diffusion_table[None, None, :], -1)
    speed_blocks = jnp.sum(onehot[:, :, :, None] * velocity_table[None, None, :, :], -2)

    def expand(lookup):
        return jnp.repeat(jnp.repeat(lookup, width_x, 0), width_y, 1)

    return (
        expand(diffusion_blocks) * roughness,
        expand(speed_blocks[..., 0]),
        expand(speed_blocks[..., 1]),
    )


def coarsen(values):
    shape_now = values.shape
    blocked = values.reshape(shape_now[:-2] + (shape_now[-2] // 2, 2, shape_now[-1] // 2, 2))
    return blocked.mean(axis=(-3, -1))


def refine(values):
    return jnp.repeat(jnp.repeat(values, 2, -2), 2, -1)


def level_down(coef):
    return (coarsen(coef[0]), 2.0 * coarsen(coef[1]), 2.0 * coarsen(coef[2]))


def advance(state_now, diffusion, speed_x, speed_y):
    east_side = jnp.roll(state_now, -1, -2)
    west_side = jnp.roll(state_now, 1, -2)
    north_side = jnp.roll(state_now, -1, -1)
    south_side = jnp.roll(state_now, 1, -1)
    laplacian = east_side + west_side + north_side + south_side - 4.0 * state_now
    return (
        state_now
        + diffusion * laplacian
        - jnp.maximum(speed_x, 0.0) * (state_now - west_side)
        - jnp.minimum(speed_x, 0.0) * (east_side - state_now)
        - jnp.maximum(speed_y, 0.0) * (state_now - south_side)
        - jnp.minimum(speed_y, 0.0) * (north_side - state_now)
    )


def sweep(start, rhs_list, coef):
    states = []
    current = start
    for offset in range(rhs_list.shape[0]):
        current = advance(current, *coef) + rhs_list[offset]
        states.append(current)
    return states


def shards(sources, initial_state, roughness, region_ids, diffusion_table, velocity_table):
    per_device = sources.shape[0]
    group_size = 4 // per_device
    inner_count = lax.axis_size("ti")
    outer_index = lax.axis_index("tb")
    inner_index = lax.axis_index("ti")
    position = inner_index % group_size
    slot_index = inner_index // group_size
    device_rank = outer_index * inner_count + inner_index
    fine_coef = coefficients(region_ids, diffusion_table, velocity_table, roughness)
    middle_coef = level_down(fine_coef)
    coarse_coef = level_down(middle_coef)
    zero_fine = jnp.zeros_like(initial_state)
    is_last = position == group_size - 1

    def run_pass(c_value):
        result = None
        states = None
        for section_pos in range(group_size):
            if section_pos == 0 and c_value is None:
                incoming = zero_fine
            else:
                outgoing = c_value if section_pos == 0 else states[-1]
                got = passed_along(outgoing, ("tb", "ti"), 1)
                incoming = (
                    jnp.where(device_rank == 0, initial_state, got) if section_pos == 0 else got
                )
            states = jnp.stack(sweep(incoming, sources, fine_coef))
            result = (
                states if section_pos == 0 else jnp.where(position == section_pos, states, result)
            )
        return result

    first_pass = run_pass(None)
    c_first = first_pass[-1]
    second_pass = run_pass(c_first)
    residual_c = second_pass[-1] - c_first
    restricted = coarsen(residual_c)
    mid_rows = restricted.shape[0]
    mid_cols = restricted.shape[1]
    piece_rows = mid_rows // group_size
    pieces = restricted.reshape(group_size, piece_rows, mid_cols)
    mine = pieces[group_size - 1]
    got = passed_along(pieces[group_size - 1 - 1], ("tb", "ti"), -1)
    mine = jnp.where(position == group_size - 1 - 1, got, mine)
    whole = lax.all_gather(mine, "ti", axis=0, tiled=True)
    rhs_middle = whole.reshape(4, mid_rows, mid_cols)
    zero_mid = jnp.zeros((mid_rows, mid_cols), jnp.float32)
    mid_first = sweep(zero_mid, rhs_middle, middle_coef)
    mid_c = mid_first[-1]
    coarse_rhs = coarsen(mid_c)

    def chain_turn(turn, state_now):
        incoming = passed_along(state_now, "tb", 1)
        return advance(incoming, *coarse_coef) + coarse_rhs

    chain_value = lax.fori_loop(0, lax.axis_size("tb") - 1, chain_turn, coarse_rhs)
    mid_fixed = refine(chain_value)
    mid_start = passed_along(mid_fixed, "tb", 1)
    mid_last = sweep(mid_start, rhs_middle, middle_coef)
    mid_all = jnp.stack([mid_last[0], mid_last[1], mid_last[2], mid_fixed])
    mid_pick = lax.dynamic_index_in_dim(mid_all, slot_index, 0, keepdims=False)
    c_fixed = c_first + refine(mid_pick)
    last_pass = run_pass(c_fixed)
    final_slot = jnp.where(is_last, c_fixed, last_pass[-1])
    return jnp.concatenate([last_pass[:-1], final_slot[None]], 0)


def solution(mesh):
    in_specs = (P(("tb", "ti"), None, None), P(), P(), P(), P(), P())
    out_specs = P(("tb", "ti"), None, None)
    return jax.shard_map(shards, mesh=mesh, in_specs=in_specs, out_specs=out_specs, check_vma=False)
```

profile of v0, /device:TPU:64, one launch (start us, length us, event | category | flops | bytes accessed | tf_op | source)
XLA Modules:
  0.0 463.5 jit_solution(9285012779683856968)
XLA Ops:
  14.9 16.0 %collective-permute-done.1 = f32[256,512]{0,1:T(8,128)S(1)} collective-permute-done((f32[256,512]{0,1:T(8,128)S(1)}, f32[256,512]{0,1:T(8,128)S(1)}, u32[]{:S(2)}, u32[]{:S(2)}) %collective-permute-start.1) | collective-permute-done | bytes 524320 | tf_op jit(solution)/shard_map/ppermute | solution.py:10
  37.4 14.4 %collective-permute-done.2 = f32[256,512]{0,1:T(8,128)S(1)} collective-permute-done((f32[256,512]{0,1:T(8,128)S(1)}, f32[256,512]{0,1:T(8,128)S(1)}, u32[]{:S(2)}, u32[]{:S(2)}) %collective-permute-start.2) | collective-permute-done | bytes 524320 | tf_op jit(solution)/shard_map/ppermute | solution.py:10
  75.1 34.8 %sub.605 = f32[128,2,256,2]{3,2,1,0:T(8,128)} reshape(f32[1,256,512]{2,1,0:T(8,128)S(1)} %copy.86) | data formatting | bytes 1048576 | tf_op jit(solution)/shard_map/sub | solution.py:106
  109.9 13.3 %reduce_sum.95 = f32[128,256]{1,0:T(8,128)S(1)} reduce(f32[128,2,256,2]{3,2,1,0:T(8,128)} %sub.605, f32[]{:T(128)} %constant.84.clone.1), dimensions={1,3}, to_apply=%region_5.6 | reduce | flops 98304 | bytes 655364 | tf_op jit(solution)/shard_map/reduce_sum | solution.py:34
  123.3 7.9 %collective-permute-start.4 = (f32[64,256]{1,0:T(8,128)S(1)}, f32[64,256]{1,0:T(8,128)S(1)}, u32[]{:S(2)}, u32[]{:S(2)}) collective-permute-start(f32[64,256]{1,0:T(8,128)S(1)} %slice.758), channel_id=1, source_target_pairs={{1,0},{2,1},{3,2},{4,3},{5,4},{6,5},{7,6},{8,7},{9,8},{10,9},{11,1... | collective-permute-start | bytes 196616 | tf_op jit(solution)/shard_map/ppermute | solution.py:10
  132.2 35.6 %reshape.90 = f32[128,2,256,2]{3,2,1,0:T(8,128)} reshape(f32[256,512]{1,0:T(8,128)} %copy.80) | data formatting | bytes 1048576 | tf_op jit(solution)/shard_map/reshape | solution.py:33
  167.8 13.2 %reduce_sum.92 = f32[128,256]{1,0:T(8,128)S(1)} reduce(f32[128,2,256,2]{3,2,1,0:T(8,128)} %reshape.90, f32[]{:T(128)} %constant.84.clone.1), dimensions={1,3}, to_apply=%region_2.3 | reduce | flops 98304 | bytes 655364 | tf_op jit(solution)/shard_map/reduce_sum | solution.py:34
  181.1 29.1 %all_gather.3 = f32[512,256]{1,0:T(8,128)S(1)} all-gather(f32[64,256]{1,0:T(8,128)S(1)} %slice_select_fusion.1), channel_id=1, replica_groups=mesh['tb'=16,'ti'=8] {'ti'}, dimensions={0}, use_global_device_ids=true | all-gather | bytes 589824 | tf_op jit(solution)/shard_map/all_gather | solution.py:115
  211.6 9.8 %reshape.91 = f32[64,2,128,2]{3,2,1,0:T(8,128)} reshape(f32[128,256]{1,0:T(8,128)S(1)} %slice_add_fusion) | data formatting | bytes 262144 | tf_op jit(solution)/shard_map/reshape | solution.py:33
  226.0 9.8 %mul.488 = f32[64,2,128,2]{3,2,1,0:T(8,128)} reshape(f32[128,256]{1,0:T(8,128)S(1)} %get-tuple-element.176) | data formatting | bytes 262144 | tf_op jit(solution)/shard_map/mul | solution.py:42
  240.3 9.8 %mul.485 = f32[64,2,128,2]{3,2,1,0:T(8,128)} reshape(f32[128,256]{1,0:T(8,128)S(1)} %get-tuple-element.178) | data formatting | bytes 262144 | tf_op jit(solution)/shard_map/mul | solution.py:42
  254.6 9.8 %div.29 = f32[64,2,128,2]{3,2,1,0:T(8,128)} reshape(f32[128,256]{1,0:T(8,128)S(1)} %get-tuple-element.179) | data formatting | bytes 262144 | tf_op jit(solution)/shard_map/div | solution.py:34
  268.9 137.9 %while.10 = (s32[]{:T(128)}, f32[64,128]{1,0:T(8,128)S(1)}, f32[64,128]{1,0:T(8,128)S(1)}, f32[64,128]{1,0:T(8,128)S(1)}, f32[64,128]{1,0:T(8,128)S(1)}, /*index=5*/f32[64,128]{1,0:T(8,128)S(1)}, s32[]{:T(128)}) while((s32[]{:T(128)}, f32[64,128]{1,0:T(8,128)S(1)}, f32[64,128]{1,0:T(8,128)S(1)}, f32[64,128]{1,0:T(8,128)S(1)}, ...), condition=%wide.region_11.12_spmd, body=%wide.region_10.11_spmd.sunk | while | flops 229378 | bytes 721013 | solution.py:126
  280.0 6.9 %collective-permute-done = f32[64,128]{1,0:T(8,128)S(1)} collective-permute-done((f32[64,128]{1,0:T(8,128)S(1)}, f32[64,128]{1,0:T(8,128)S(1)}, u32[]{:S(2)}, u32[]{:S(2)}) %collective-permute-start) | collective-permute-done | bytes 32800 | tf_op jit(solution)/shard_map/while/body/eval_jaxpr/ppermute | solution.py:10
  289.2 6.9 %collective-permute-done = f32[64,128]{1,0:T(8,128)S(1)} collective-permute-done((f32[64,128]{1,0:T(8,128)S(1)}, f32[64,128]{1,0:T(8,128)S(1)}, u32[]{:S(2)}, u32[]{:S(2)}) %collective-permute-start) | collective-permute-done | bytes 32800 | tf_op jit(solution)/shard_map/while/body/eval_jaxpr/ppermute | solution.py:10
  334.9 6.9 %collective-permute-done = f32[64,128]{1,0:T(8,128)S(1)} collective-permute-done((f32[64,128]{1,0:T(8,128)S(1)}, f32[64,128]{1,0:T(8,128)S(1)}, u32[]{:S(2)}, u32[]{:S(2)}) %collective-permute-start) | collective-permute-done | bytes 32800 | tf_op jit(solution)/shard_map/while/body/eval_jaxpr/ppermute | solution.py:10
  344.0 6.9 %collective-permute-done = f32[64,128]{1,0:T(8,128)S(1)} collective-permute-done((f32[64,128]{1,0:T(8,128)S(1)}, f32[64,128]{1,0:T(8,128)S(1)}, u32[]{:S(2)}, u32[]{:S(2)}) %collective-permute-start) | collective-permute-done | bytes 32800 | tf_op jit(solution)/shard_map/while/body/eval_jaxpr/ppermute | solution.py:10
  353.2 6.9 %collective-permute-done = f32[64,128]{1,0:T(8,128)S(1)} collective-permute-done((f32[64,128]{1,0:T(8,128)S(1)}, f32[64,128]{1,0:T(8,128)S(1)}, u32[]{:S(2)}, u32[]{:S(2)}) %collective-permute-start) | collective-permute-done | bytes 32800 | tf_op jit(solution)/shard_map/while/body/eval_jaxpr/ppermute | solution.py:10
  380.6 7.3 %collective-permute-done = f32[64,128]{1,0:T(8,128)S(1)} collective-permute-done((f32[64,128]{1,0:T(8,128)S(1)}, f32[64,128]{1,0:T(8,128)S(1)}, u32[]{:S(2)}, u32[]{:S(2)}) %collective-permute-start) | collective-permute-done | bytes 32800 | tf_op jit(solution)/shard_map/while/body/eval_jaxpr/ppermute | solution.py:10
  390.1 6.9 %collective-permute-done = f32[64,128]{1,0:T(8,128)S(1)} collective-permute-done((f32[64,128]{1,0:T(8,128)S(1)}, f32[64,128]{1,0:T(8,128)S(1)}, u32[]{:S(2)}, u32[]{:S(2)}) %collective-permute-start) | collective-permute-done | bytes 32800 | tf_op jit(solution)/shard_map/while/body/eval_jaxpr/ppermute | solution.py:10
  399.3 7.3 %collective-permute-done = f32[64,128]{1,0:T(8,128)S(1)} collective-permute-done((f32[64,128]{1,0:T(8,128)S(1)}, f32[64,128]{1,0:T(8,128)S(1)}, u32[]{:S(2)}, u32[]{:S(2)}) %collective-permute-start) | collective-permute-done | bytes 32800 | tf_op jit(solution)/shard_map/while/body/eval_jaxpr/ppermute | solution.py:10
  409.4 7.6 %collective-permute-done.5 = f32[128,256]{1,0:T(8,128)S(1)} collective-permute-done((f32[128,256]{1,0:T(8,128)S(1)}, f32[128,256]{1,0:T(8,128)S(1)}, u32[]{:S(2)}, u32[]{:S(2)}) %collective-permute-start.5) | collective-permute-done | bytes 131104 | tf_op jit(solution)/shard_map/ppermute | solution.py:10
  424.0 15.5 %collective-permute-done.6 = f32[256,512]{0,1:T(8,128)S(1)} collective-permute-done((f32[256,512]{0,1:T(8,128)S(1)}, f32[256,512]{0,1:T(8,128)S(1)}, u32[]{:S(2)}, u32[]{:S(2)}) %collective-permute-start.6) | collective-permute-done | bytes 524320 | tf_op jit(solution)/shard_map/ppermute | solution.py:10
  446.6 12.0 %collective-permute-done.7 = f32[256,512]{0,1:T(8,128)S(1)} collective-permute-done((f32[256,512]{0,1:T(8,128)}, f32[256,512]{0,1:T(8,128)S(1)}, u32[]{:S(2)}, u32[]{:S(2)}) %collective-permute-start.7) | collective-permute-done | bytes 524320 | tf_op jit(solution)/shard_map/ppermute | solution.py:10
  (273 shorter events, 167.2 us)
Async XLA Ops:
  11.5 21.6 %copy-start.3 = (f32[256,512]{0,1:T(8,128)}, f32[256,512]{0,1:T(8,128)S(1)}, u32[]{:S(2)}) copy-start(f32[256,512]{0,1:T(8,128)S(1)} %fusion.9) | copy-start | bytes 1572868
  11.5 19.4 %collective-permute-start.1 = (f32[256,512]{0,1:T(8,128)S(1)}, f32[256,512]{0,1:T(8,128)S(1)}, u32[]{:S(2)}, u32[]{:S(2)}) collective-permute-start(f32[256,512]{0,1:T(8,128)S(1)} %fusion.9), channel_id=1, source_target_pairs={{0,1},{1,2},{2,3},{3,4},{4,5},{5,6},{6,7},{7,8},{8,9},{9,10},{10,1... | collective-permute-start | bytes 1572872 | tf_op jit(solution)/shard_map/ppermute | solution.py:10
  34.2 17.6 %collective-permute-start.2 = (f32[256,512]{0,1:T(8,128)S(1)}, f32[256,512]{0,1:T(8,128)S(1)}, u32[]{:S(2)}, u32[]{:S(2)}) collective-permute-start(f32[256,512]{0,1:T(8,128)S(1)} %bitcast.304), channel_id=1, source_target_pairs={{0,1},{1,2},{2,3},{3,4},{4,5},{5,6},{6,7},{7,8},{8,9},{9,10},{10,1... | collective-permute-start | bytes 1572872 | tf_op jit(solution)/shard_map/ppermute | solution.py:10
  54.8 16.8 %collective-permute-start.3 = (f32[256,512]{0,1:T(8,128)}, f32[256,512]{0,1:T(8,128)S(1)}, u32[]{:S(2)}, u32[]{:S(2)}) collective-permute-start(f32[256,512]{0,1:T(8,128)} %fusion.29), channel_id=1, source_target_pairs={{0,1},{1,2},{2,3},{3,4},{4,5},{5,6},{6,7},{7,8},{8,9},{9,10},{10,1... | collective-permute-start | bytes 1572872 | tf_op jit(solution)/shard_map/ppermute | solution.py:10
  109.9 21.2 %copy-start.5 = (f32[128,2,256]{2,0,1:T(8,128)S(1)}, f32[128,2,256]{2,0,1:T(8,128)}, u32[]{:S(2)}) copy-start(f32[128,2,256]{2,0,1:T(8,128)} %copy.84) | copy-start | bytes 786436
  123.3 57.8 %collective-permute-start.4 = (f32[64,256]{1,0:T(8,128)S(1)}, f32[64,256]{1,0:T(8,128)S(1)}, u32[]{:S(2)}, u32[]{:S(2)}) collective-permute-start(f32[64,256]{1,0:T(8,128)S(1)} %slice.758), channel_id=1, source_target_pairs={{1,0},{2,1},{3,2},{4,3},{5,4},{6,5},{7,6},{8,7},{9,8},{10,9},{11,1... | collective-permute-start | bytes 196616 | tf_op jit(solution)/shard_map/ppermute | solution.py:10
  268.9 8.8 %collective-permute-start = (f32[64,128]{1,0:T(8,128)S(1)}, f32[64,128]{1,0:T(8,128)S(1)}, u32[]{:S(2)}, u32[]{:S(2)}) collective-permute-start(f32[64,128]{1,0:T(8,128)S(1)} %get-tuple-element.275), channel_id=1, source_target_pairs={{0,8},{8,16},{16,24},{24,32},{32,40},{40,48},{48,56},{56,64},{64,7... | collective-permute-start | bytes 98312 | tf_op jit(solution)/shard_map/while/body/eval_jaxpr/ppermute | solution.py:10
  278.1 8.8 %collective-permute-start = (f32[64,128]{1,0:T(8,128)S(1)}, f32[64,128]{1,0:T(8,128)S(1)}, u32[]{:S(2)}, u32[]{:S(2)}) collective-permute-start(f32[64,128]{1,0:T(8,128)S(1)} %get-tuple-element.275), channel_id=1, source_target_pairs={{0,8},{8,16},{16,24},{24,32},{32,40},{40,48},{48,56},{56,64},{64,7... | collective-permute-start | bytes 98312 | tf_op jit(solution)/shard_map/while/body/eval_jaxpr/ppermute | solution.py:10
  287.2 8.8 %collective-permute-start = (f32[64,128]{1,0:T(8,128)S(1)}, f32[64,128]{1,0:T(8,128)S(1)}, u32[]{:S(2)}, u32[]{:S(2)}) collective-permute-start(f32[64,128]{1,0:T(8,128)S(1)} %get-tuple-element.275), channel_id=1, source_target_pairs={{0,8},{8,16},{16,24},{24,32},{32,40},{40,48},{48,56},{56,64},{64,7... | collective-permute-start | bytes 98312 | tf_op jit(solution)/shard_map/while/body/eval_jaxpr/ppermute | solution.py:10
  296.4 8.8 %collective-permute-start = (f32[64,128]{1,0:T(8,128)S(1)}, f32[64,128]{1,0:T(8,128)S(1)}, u32[]{:S(2)}, u32[]{:S(2)}) collective-permute-start(f32[64,128]{1,0:T(8,128)S(1)} %get-tuple-element.275), channel_id=1, source_target_pairs={{0,8},{8,16},{16,24},{24,32},{32,40},{40,48},{48,56},{56,64},{64,7... | collective-permute-start | bytes 98312 | tf_op jit(solution)/shard_map/while/body/eval_jaxpr/ppermute | solution.py:10
  305.5 8.8 %collective-permute-start = (f32[64,128]{1,0:T(8,128)S(1)}, f32[64,128]{1,0:T(8,128)S(1)}, u32[]{:S(2)}, u32[]{:S(2)}) collective-permute-start(f32[64,128]{1,0:T(8,128)S(1)} %get-tuple-element.275), channel_id=1, source_target_pairs={{0,8},{8,16},{16,24},{24,32},{32,40},{40,48},{48,56},{56,64},{64,7... | collective-permute-start | bytes 98312 | tf_op jit(solution)/shard_map/while/body/eval_jaxpr/ppermute | solution.py:10
  314.7 8.8 %collective-permute-start = (f32[64,128]{1,0:T(8,128)S(1)}, f32[64,128]{1,0:T(8,128)S(1)}, u32[]{:S(2)}, u32[]{:S(2)}) collective-permute-start(f32[64,128]{1,0:T(8,128)S(1)} %get-tuple-element.275), channel_id=1, source_target_pairs={{0,8},{8,16},{16,24},{24,32},{32,40},{40,48},{48,56},{56,64},{64,7... | collective-permute-start | bytes 98312 | tf_op jit(solution)/shard_map/while/body/eval_jaxpr/ppermute | solution.py:10
  323.8 8.8 %collective-permute-start = (f32[64,128]{1,0:T(8,128)S(1)}, f32[64,128]{1,0:T(8,128)S(1)}, u32[]{:S(2)}, u32[]{:S(2)}) collective-permute-start(f32[64,128]{1,0:T(8,128)S(1)} %get-tuple-element.275), channel_id=1, source_target_pairs={{0,8},{8,16},{16,24},{24,32},{32,40},{40,48},{48,56},{56,64},{64,7... | collective-permute-start | bytes 98312 | tf_op jit(solution)/shard_map/while/body/eval_jaxpr/ppermute | solution.py:10
  333.0 8.8 %collective-permute-start = (f32[64,128]{1,0:T(8,128)S(1)}, f32[64,128]{1,0:T(8,128)S(1)}, u32[]{:S(2)}, u32[]{:S(2)}) collective-permute-start(f32[64,128]{1,0:T(8,128)S(1)} %get-tuple-element.275), channel_id=1, source_target_pairs={{0,8},{8,16},{16,24},{24,32},{32,40},{40,48},{48,56},{56,64},{64,7... | collective-permute-start | bytes 98312 | tf_op jit(solution)/shard_map/while/body/eval_jaxpr/ppermute | solution.py:10
  342.1 8.8 %collective-permute-start = (f32[64,128]{1,0:T(8,128)S(1)}, f32[64,128]{1,0:T(8,128)S(1)}, u32[]{:S(2)}, u32[]{:S(2)}) collective-permute-start(f32[64,128]{1,0:T(8,128)S(1)} %get-tuple-element.275), channel_id=1, source_target_pairs={{0,8},{8,16},{16,24},{24,32},{32,40},{40,48},{48,56},{56,64},{64,7... | collective-permute-start | bytes 98312 | tf_op jit(solution)/shard_map/while/body/eval_jaxpr/ppermute | solution.py:10
  351.3 8.8 %collective-permute-start = (f32[64,128]{1,0:T(8,128)S(1)}, f32[64,128]{1,0:T(8,128)S(1)}, u32[]{:S(2)}, u32[]{:S(2)}) collective-permute-start(f32[64,128]{1,0:T(8,128)S(1)} %get-tuple-element.275), channel_id=1, source_target_pairs={{0,8},{8,16},{16,24},{24,32},{32,40},{40,48},{48,56},{56,64},{64,7... | collective-permute-start | bytes 98312 | tf_op jit(solution)/shard_map/while/body/eval_jaxpr/ppermute | solution.py:10
  360.4 8.8 %collective-permute-start = (f32[64,128]{1,0:T(8,128)S(1)}, f32[64,128]{1,0:T(8,128)S(1)}, u32[]{:S(2)}, u32[]{:S(2)}) collective-permute-start(f32[64,128]{1,0:T(8,128)S(1)} %get-tuple-element.275), channel_id=1, source_target_pairs={{0,8},{8,16},{16,24},{24,32},{32,40},{40,48},{48,56},{56,64},{64,7... | collective-permute-start | bytes 98312 | tf_op jit(solution)/shard_map/while/body/eval_jaxpr/ppermute | solution.py:10
  369.5 8.8 %collective-permute-start = (f32[64,128]{1,0:T(8,128)S(1)}, f32[64,128]{1,0:T(8,128)S(1)}, u32[]{:S(2)}, u32[]{:S(2)}) collective-permute-start(f32[64,128]{1,0:T(8,128)S(1)} %get-tuple-element.275), channel_id=1, source_target_pairs={{0,8},{8,16},{16,24},{24,32},{32,40},{40,48},{48,56},{56,64},{64,7... | collective-permute-start | bytes 98312 | tf_op jit(solution)/shard_map/while/body/eval_jaxpr/ppermute | solution.py:10
  378.7 9.2 %collective-permute-start = (f32[64,128]{1,0:T(8,128)S(1)}, f32[64,128]{1,0:T(8,128)S(1)}, u32[]{:S(2)}, u32[]{:S(2)}) collective-permute-start(f32[64,128]{1,0:T(8,128)S(1)} %get-tuple-element.275), channel_id=1, source_target_pairs={{0,8},{8,16},{16,24},{24,32},{32,40},{40,48},{48,56},{56,64},{64,7... | collective-permute-start | bytes 98312 | tf_op jit(solution)/shard_map/while/body/eval_jaxpr/ppermute | solution.py:10
  388.2 8.8 %collective-permute-start = (f32[64,128]{1,0:T(8,128)S(1)}, f32[64,128]{1,0:T(8,128)S(1)}, u32[]{:S(2)}, u32[]{:S(2)}) collective-permute-start(f32[64,128]{1,0:T(8,128)S(1)} %get-tuple-element.275), channel_id=1, source_target_pairs={{0,8},{8,16},{16,24},{24,32},{32,40},{40,48},{48,56},{56,64},{64,7... | collective-permute-start | bytes 98312 | tf_op jit(solution)/shard_map/while/body/eval_jaxpr/ppermute | solution.py:10
  397.3 9.2 %collective-permute-start = (f32[64,128]{1,0:T(8,128)S(1)}, f32[64,128]{1,0:T(8,128)S(1)}, u32[]{:S(2)}, u32[]{:S(2)}) collective-permute-start(f32[64,128]{1,0:T(8,128)S(1)} %get-tuple-element.275), channel_id=1, source_target_pairs={{0,8},{8,16},{16,24},{24,32},{32,40},{40,48},{48,56},{56,64},{64,7... | collective-permute-start | bytes 98312 | tf_op jit(solution)/shard_map/while/body/eval_jaxpr/ppermute | solution.py:10
  407.1 9.9 %collective-permute-start.5 = (f32[128,256]{1,0:T(8,128)S(1)}, f32[128,256]{1,0:T(8,128)S(1)}, u32[]{:S(2)}, u32[]{:S(2)}) collective-permute-start(f32[128,256]{1,0:T(8,128)S(1)} %copy.88), channel_id=1, source_target_pairs={{0,8},{8,16},{16,24},{24,32},{32,40},{40,48},{48,56},{56,64},{64,7... | collective-permute-start | bytes 393224 | tf_op jit(solution)/shard_map/ppermute | solution.py:10
  422.1 17.4 %collective-permute-start.6 = (f32[256,512]{0,1:T(8,128)S(1)}, f32[256,512]{0,1:T(8,128)S(1)}, u32[]{:S(2)}, u32[]{:S(2)}) collective-permute-start(f32[256,512]{0,1:T(8,128)S(1)} %bitcast_add_fusion), channel_id=1, source_target_pairs={{0,1},{1,2},{2,3},{3,4},{4,5},{5,6},{6,7},{7,8},{8,9},{9,10},{10,1... | collective-permute-start | bytes 1572872 | tf_op jit(solution)/shard_map/ppermute | solution.py:10
  442.5 16.1 %collective-permute-start.7 = (f32[256,512]{0,1:T(8,128)}, f32[256,512]{0,1:T(8,128)S(1)}, u32[]{:S(2)}, u32[]{:S(2)}) collective-permute-start(f32[256,512]{0,1:T(8,128)} %fusion.49), channel_id=1, source_target_pairs={{0,1},{1,2},{2,3},{3,4},{4,5},{5,6},{6,7},{7,8},{8,9},{9,10},{10,1... | collective-permute-start | bytes 1572872 | tf_op jit(solution)/shard_map/ppermute | solution.py:10
  (4 other events, 37.5 us)
where the time goes:
time: 465 us; the launch traced here: 464 us
  waiting for transfers between devices  170 us (37%)
  local copies, waits for them, and re-layouts  146 us (31%)
  other arithmetic  66.8 us (14%)
  starting transfers between devices  50.1 us (11%)
  blocking collectives  29.1 us (6%)
    ppermute x22, waiting for transfers between devices, passed_along(): lax.ppermute(value, axis, [(source, source + steps) for source in range(i...  170 us
    ppermute x22, starting transfers between devices, passed_along(): lax.ppermute(value, axis, [(source, source + steps) for source in range(i...  50.1 us
    reshape x2, local copies, waits for them, and re-layouts, coarsen(): values.reshape(shape_now[:-2] + (shape_now[-2] // 2, 2, shape_now[-1] //...  45.4 us
    reduce_sum x7, other arithmetic, coarsen(): return blocked.mean(axis=(-3, -1))  44.7 us
    sub x2, local copies, waits for them, and re-layouts, shards(): residual_c = second_pass[-1] - c_first  35 us
    all_gather x1, blocking collectives, shards(): whole = lax.all_gather(mine, 'ti', axis=0, tiled=True)  29.1 us
    mul x2, local copies, waits for them, and re-layouts, level_down(): return (coarsen(coef[0]), 2.0 * coarsen(coef[1]), 2.0 * coarsen(coef[2]))  19.6 us
    broadcast_in_dim x9, local copies, waits for them, and re-layouts, expand(): return jnp.repeat(jnp.repeat(lookup, width_x, 0), width_y, 1)  14.1 us
  transfers between devices with their start and end apart: 22, of which 20 were waited for; matrix products, arithmetic and copies ran while one was open for 15% of the time, Pallas kernels for 0%

commit v1 on v0

v1 whole, which is shorter than its diff:
```python
import functools

import jax
import jax.numpy as jnp
from jax import lax
from jax.experimental import pallas as pl
from jax.experimental.pallas import tpu as pltpu
from jax.sharding import PartitionSpec as P

MESH = pl.DeviceIdType.MESH
F32 = jnp.float32
BF16 = jnp.bfloat16
CHUNKS = 4


def wrap(ref, rows):
    ref[0] = pltpu.roll(ref[rows], 1, 0)
    ref[rows + 1] = pltpu.roll(ref[1], 7, 0)


def stencil(coef, r, centre, west, east):
    width = centre.shape[-1]
    south = pltpu.roll(centre, 1, 1)
    north = pltpu.roll(centre, width - 1, 1)
    return (
        (coef[0, r] * centre + coef[1, r] * west)
        + coef[2, r] * east
        + (coef[3, r] * south + coef[4, r] * north)
    )


def propagate(src, coef, rows, emit):
    wrap(src, rows)
    for r in range(rows):
        emit(r, stencil(coef, r, src[r + 1], src[r], src[r + 2]))


def into(dst):
    def emit(r, value):
        dst[r + 1] = value

    return emit


def exact_dot(x, matrix):
    first = x.astype(BF16)
    rest = x - first.astype(F32)
    second = rest.astype(BF16)
    third = (rest - second.astype(F32)).astype(BF16)

    def dot(part):
        return jnp.dot(part, matrix, preferred_element_type=F32)

    return dot(first) + (dot(second) + dot(third))


def pair_rows(value):
    rows, eight, width = value.shape
    halves = value.reshape(rows // 2, 2, eight, width)
    return halves[:, 0] + halves[:, 1]


def coarsen(value, matrix):
    rows, eight, width = value.shape
    summed = pair_rows(value).reshape(rows // 2 * eight, width)
    return exact_dot(summed, matrix).reshape(rows // 2, eight, width // 2)


def refine_lanes(value, matrix):
    rows, eight, width = value.shape
    return exact_dot(value.reshape(rows * eight, width), matrix).reshape(rows, eight, width * 2)


def put_refined(dst, value, matrix):
    wide = refine_lanes(value, matrix)
    for r in range(value.shape[0]):
        dst[2 * r + 1] = wide[r]
        dst[2 * r + 2] = wide[r]


def set_coefficients(coef, r, diffusion, speed_x, speed_y):
    coef[0, r] = 1.0 - 4.0 * diffusion - jnp.abs(speed_x) - jnp.abs(speed_y)
    coef[1, r] = diffusion + jnp.maximum(speed_x, 0.0)
    coef[2, r] = diffusion - jnp.minimum(speed_x, 0.0)
    coef[3, r] = diffusion + jnp.maximum(speed_y, 0.0)
    coef[4, r] = diffusion - jnp.minimum(speed_y, 0.0)


def block_matrix(rows, columns, wide_rows, entry):
    row = lax.broadcasted_iota(jnp.int32, (rows, columns), 0)
    column = lax.broadcasted_iota(jnp.int32, (rows, columns), 1)
    same = (row // 2 == column) if wide_rows else (row == column // 2)
    return jnp.where(same, entry, 0.0).astype(BF16)


def kernel(
    src, start, rough, ids, diffusion_table, velocity_table, out,
    raw, maps, ids_wide, coef0, coef1, coef2, down1, down2, up1, up0,
    rhs, y, work, tmid, c_own, y_in, c_in, third, beta, beta_in, mid_own, mid_in, level1, e_own, e_in, g_own, g_in,
    out_raw, in_sem, out_sem, y_send, y_recv, c_send, c_recv, b_send, b_recv, m_send, m_recv, e_send, e_recv, g_send, g_recv,
):
    tb, ti = lax.axis_index("tb"), lax.axis_index("ti")
    outer = lax.axis_size("tb")
    odd = lax.rem(ti, 2) == 1
    even = lax.rem(ti, 2) == 0
    slot = ti // 2
    first_interval = (tb == 0) & (slot == 0)
    last_interval = (tb == outer - 1) & (slot == 3)
    next_tb = lax.rem(tb + jnp.where(slot == 3, 1, 0), outer)
    next_even = lax.rem(ti - lax.rem(ti, 2) + 2, 8)
    width = 512

    barrier = pltpu.get_barrier_semaphore()
    for d in range(8):
        from_tb = lax.rem(tb + (outer - 1 if d >= 6 else 0), outer)

        @pl.when((from_tb != tb) | (ti != d))
        def _():
            pl.semaphore_signal(barrier, 1, device_id=(from_tb, d), device_id_type=MESH)

    @pl.when(ti == 7)
    def _():
        pl.semaphore_signal(barrier, 1, device_id=(tb, 6), device_id_type=MESH)

    for d in range(1, 16):

        @pl.when(tb - d >= 0)
        def _():
            pl.semaphore_signal(barrier, 1, device_id=(tb - d, ti), device_id_type=MESH)

    def load(index, array, part):
        return [
            pltpu.make_async_copy(
                array.at[:, pl.ds(128 * t, 128)] if part is None else array.at[part, :, pl.ds(128 * t, 128)],
                raw.at[index, t],
                in_sem.at[index, t],
            )
            for t in range(4)
        ]

    loads = [load(0, rough, None), load(1, src, 0), load(2, src, 1), load(3, start, None)]
    for group in loads:
        for copy in group:
            copy.start()

    def raw_row(index, r):
        return jnp.concatenate([raw[index, t, pl.ds(r, 8, stride=32), :] for t in range(4)], axis=1)

    down1[...] = block_matrix(512, 256, True, 0.25)
    down2[...] = block_matrix(256, 128, True, 0.25)
    up1[...] = block_matrix(128, 256, False, 1.0)
    up0[...] = block_matrix(256, 512, False, 1.0)

    ids_wide[...] = jnp.full(ids_wide.shape, -1, jnp.int32)
    ids_wide[:, 0:16] = ids[...]
    kinds = jnp.concatenate([ids_wide[pl.ds(h, 8, stride=2), :] for h in range(2)], axis=0)
    tables = [jnp.zeros(kinds.shape, F32) for _ in range(3)]
    for kind in range(16):
        hit = kinds == kind
        for which, entry in enumerate((diffusion_table[kind], velocity_table[kind, 0], velocity_table[kind, 1])):
            tables[which] = jnp.where(hit, entry, tables[which])

    def spread(cells, scale):
        column = lax.broadcasted_iota(jnp.int32, (128, 16 * cells), 0)
        cell = lax.broadcasted_iota(jnp.int32, (128, 16 * cells), 1)
        return jnp.where(cell // cells == column, scale, 0.0).astype(F32)

    stacked = jnp.concatenate(tables, axis=0)

    def expand(rows, cells, scale):
        return jnp.dot(rows, spread(cells, scale), precision=lax.Precision.HIGHEST, preferred_element_type=F32)

    maps[...] = expand(stacked, 32, 1.0)
    speeds1 = expand(stacked[16:], 16, 2.0)
    speeds2 = expand(stacked[16:], 8, 4.0)

    for copy in loads[0]:
        copy.wait()
    for r in range(32):
        h = r // 16
        diffusion = maps[8 * h : 8 * h + 8] * raw_row(0, r)
        tmid[r] = diffusion
        set_coefficients(coef0, r, diffusion, maps[16 + 8 * h : 24 + 8 * h], maps[32 + 8 * h : 40 + 8 * h])
    diffusion1 = coarsen(tmid[...], down1[...])
    for r in range(16):
        h = r // 8
        set_coefficients(coef1, r, diffusion1[r], speeds1[8 * h : 8 * h + 8], speeds1[16 + 8 * h : 24 + 8 * h])
    diffusion2 = coarsen(diffusion1, down2[...])
    for r in range(8):
        h = r // 4
        set_coefficients(coef2, r, diffusion2[r], speeds2[8 * h : 8 * h + 8], speeds2[16 + 8 * h : 24 + 8 * h])

    for group in loads[1:]:
        for copy in group:
            copy.wait()
    for r in range(32):
        rhs[0, r + 1] = raw_row(1, r)
        rhs[1, r + 1] = raw_row(2, r)

    def add_second(r, value):
        total = value + rhs[1, r + 1]
        y[r + 1] = total

    propagate(rhs.at[0], coef0, 32, add_second)

    pl.semaphore_wait(barrier, jnp.where(ti < 6, 7, jnp.where(ti == 6, 9, 8)) + outer - 1 - tb)

    chunk = 32 // CHUNKS

    def y_copy(c):
        return pltpu.make_async_remote_copy(
            src_ref=y.at[pl.ds(1 + c * chunk, chunk)],
            dst_ref=y_in.at[pl.ds(1 + c * chunk, chunk)],
            send_sem=y_send.at[c],
            recv_sem=y_recv.at[c],
            device_id=(tb, ti + 1),
            device_id_type=MESH,
        )

    @pl.when(even)
    def _():
        for c in range(CHUNKS):
            y_copy(c).start()

    for r in range(32):
        initial = raw_row(3, r)
        work[0, r + 1] = jnp.where(last_interval, jnp.where(odd, initial, 0.0), y[r + 1])

        @pl.when(first_interval)
        def _():
            c_in[r] = initial

    def turn(i, carry):
        propagate(work.at[lax.rem(i, 2)], coef0, 32, into(work.at[1 - lax.rem(i, 2)]))
        return carry

    lax.fori_loop(0, jnp.where(odd, 4, 6), turn, 0)
    beta[...] = coarsen(work[0, 1:33], down1[...])

    next_slot = lax.rem(slot + 1, 4)

    def beta_copy(target):
        return pltpu.make_async_remote_copy(
            src_ref=beta,
            dst_ref=beta_in.at[2 * next_slot + lax.rem(ti, 2)],
            send_sem=b_send.at[target],
            recv_sem=b_recv.at[2 * next_slot + lax.rem(ti, 2)],
            device_id=(next_tb, 2 * target + 1),
            device_id_type=MESH,
        )

    for target in range(3):

        @pl.when(next_slot <= target)
        def _():
            beta_copy(target).start()

    def level1_turn(i, carry):
        propagate(level1.at[lax.rem(i, 2)], coef1, 16, into(level1.at[1 - lax.rem(i, 2)]))
        return carry

    level1[0, 1:17] = beta[...]
    count = 3 - next_slot
    lax.fori_loop(0, count, level1_turn, 0)
    e_own[...] = coarsen(level1[lax.rem(count, 2), 1:17], down2[...])

    def e_copy(target):
        return pltpu.make_async_remote_copy(
            src_ref=e_own,
            dst_ref=e_in.at[ti],
            send_sem=e_send.at[target],
            recv_sem=e_recv.at[ti],
            device_id=(next_tb, target),
            device_id_type=MESH,
        )

    for target in range(8):

        @pl.when((ti != target) | (next_tb != tb))
        def _():
            e_copy(target).start()

        @pl.when((ti == target) & (next_tb == tb))
        def _():
            e_in[target] = e_own[...]

    def e_arrival(source):
        return pltpu.make_async_remote_copy(
            src_ref=e_own,
            dst_ref=e_in.at[source],
            send_sem=e_send.at[source],
            recv_sem=e_recv.at[source],
            device_id=(tb, source),
            device_id_type=MESH,
        )

    for source in range(8):

        @pl.when((ti != source) | (source >= 6))
        def _():
            e_arrival(source).wait_recv()

    total = e_in[0]
    for source in range(1, 8):
        total = total + e_in[source]
    g_own[...] = total

    def g_copy(d):
        return pltpu.make_async_remote_copy(
            src_ref=g_own,
            dst_ref=g_in.at[tb],
            send_sem=g_send.at[d],
            recv_sem=g_recv.at[tb],
            device_id=(tb + d, ti),
            device_id_type=MESH,
        )

    for d in range(1, 16):

        @pl.when(tb + d < outer)
        def _():
            g_copy(d).start()

    def c_copy(c, target):
        return pltpu.make_async_remote_copy(
            src_ref=c_own.at[pl.ds(c * chunk, chunk)],
            dst_ref=c_in.at[pl.ds(c * chunk, chunk)],
            send_sem=c_send.at[2 * c + target],
            recv_sem=c_recv.at[c],
            device_id=(next_tb, next_even + target),
            device_id_type=MESH,
        )

    def mid_copy(target):
        return pltpu.make_async_remote_copy(
            src_ref=mid_own,
            dst_ref=mid_in,
            send_sem=m_send.at[target],
            recv_sem=m_recv,
            device_id=(tb, next_even + target),
            device_id_type=MESH,
        )

    def beta_arrival(which):
        return pltpu.make_async_remote_copy(
            src_ref=beta,
            dst_ref=beta_in.at[which],
            send_sem=b_send.at[0],
            recv_sem=b_recv.at[which],
            device_id=(tb, ti - 1),
            device_id_type=MESH,
        )

    @pl.when(odd)
    def _():
        for c in range(CHUNKS):
            y_copy(c).wait_recv()

        def emit_first(r, value):
            work[0, r + 1] = value
            third[r] = value + rhs[0, r + 1]

        propagate(y_in, coef0, 32, emit_first)

        def emit_second(r, value):
            c_own[r] = value + y[r + 1]

        propagate(work.at[0], coef0, 32, emit_second)

        @pl.when(jnp.logical_not(last_interval))
        def _():
            for c in range(CHUNKS):
                for target in range(2):
                    c_copy(c, target).start()

    @pl.when(odd & (slot < 3))
    def _():
        for which in range(2):
            beta_arrival(which).wait_recv()
        level1[0, 1:17] = beta_in[0] + beta_in[1]

        def mid_turn(i, carry):
            for which in range(2):
                beta_arrival(2 * i + which).wait_recv()

            def emit(r, value):
                level1[lax.rem(i, 2), r + 1] = value + (beta_in[2 * i, r] + beta_in[2 * i + 1, r])

            propagate(level1.at[lax.rem(i + 1, 2)], coef1, 16, emit)
            return carry

        lax.fori_loop(1, slot + 1, mid_turn, 0)
        mid_own[...] = level1[lax.rem(slot, 2), 1:17]
        for target in range(2):
            mid_copy(target).start()

    @pl.when(slot == 0)
    def _():
        mid_in[...] = jnp.zeros(mid_in.shape, F32)

    def level2(value):
        first = pltpu.roll(value[7], 1, 0)
        last = pltpu.roll(value[0], 7, 0)
        rows = [first] + [value[r] for r in range(8)] + [last]
        return jnp.stack([stencil(coef2, r, rows[r + 1], rows[r], rows[r + 2]) for r in range(8)])

    def g_arrival(source):
        return pltpu.make_async_remote_copy(
            src_ref=g_own,
            dst_ref=g_in.at[source],
            send_sem=g_send.at[0],
            recv_sem=g_recv.at[source],
            device_id=(0, ti),
            device_id_type=MESH,
        )

    def chain_turn(source, state):
        g_arrival(source).wait_recv()
        return level2(state) + g_in[source]

    before = lax.fori_loop(0, tb, chain_turn, jnp.zeros((8, 8, 128), F32))
    g_in[tb] = level2(before) + g_own[...]

    put_refined(level1.at[0], before, up1[...])
    lax.fori_loop(0, slot, level1_turn, 0)
    here = lax.rem(slot, 2)

    @pl.when(slot > 0)
    def _():
        mid_copy(0).wait_recv()

    @pl.when(jnp.logical_not(first_interval))
    def _():
        for c in range(CHUNKS):
            c_copy(c, 0).wait_recv()

    wide = refine_lanes(level1[here, 1:17] + mid_in[...], up0[...])
    for r in range(32):
        work[0, r + 1] = c_in[r] + wide[r // 2]

    def put_out(index, r, value):
        for t in range(4):
            out_raw[index, t, pl.ds(r, 8, stride=32), :] = value[:, 128 * t : 128 * t + 128]

    def out_copies(index):
        return [
            pltpu.make_async_copy(out_raw.at[index, t], out.at[index, :, pl.ds(128 * t, 128)], out_sem.at[index, t])
            for t in range(4)
        ]

    @pl.when(even)
    def _():
        def emit_first(r, value):
            state = value + rhs[0, r + 1]
            work[1, r + 1] = state
            put_out(0, r, state)

        propagate(work.at[0], coef0, 32, emit_first)
        for copy in out_copies(0):
            copy.start()

        def emit_second(r, value):
            put_out(1, r, value + rhs[1, r + 1])

        propagate(work.at[1], coef0, 32, emit_second)

    @pl.when(odd)
    def _():
        propagate(work.at[0], coef0, 32, into(work.at[1]))
        propagate(work.at[1], coef0, 32, into(work.at[0]))

        def emit(r, value):
            put_out(0, r, value + third[r])

        propagate(work.at[0], coef0, 32, emit)
        for copy in out_copies(0):
            copy.start()

        @pl.when(slot < 3)
        def _():
            def emit_end(r, value):
                mid_own_end[r] = value + mid_own[r]

            mid_own_end = beta_in.at[7]
            propagate(level1.at[here], coef1, 16, emit_end)

        @pl.when(slot == 3)
        def _():
            fixed = refine_lanes(g_in[tb], up1[...])
            for r in range(16):
                beta_in[7, r] = fixed[r // 2]

        wide = refine_lanes(beta_in[7], up0[...])
        for r in range(32):
            put_out(1, r, c_own[r] + wide[r // 2])

    for copy in out_copies(1):
        copy.start()

    @pl.when(even)
    def _():
        for c in range(CHUNKS):
            y_copy(c).wait_send()

    for target in range(3):

        @pl.when(next_slot <= target)
        def _():
            beta_copy(target).wait_send()

    for target in range(8):

        @pl.when((ti != target) | (next_tb != tb))
        def _():
            e_copy(target).wait_send()

    for d in range(1, 16):

        @pl.when(tb + d < outer)
        def _():
            g_copy(d).wait_send()

    @pl.when(odd & jnp.logical_not(last_interval))
    def _():
        for c in range(CHUNKS):
            for target in range(2):
                c_copy(c, target).wait_send()

    @pl.when(odd & (slot < 3))
    def _():
        for target in range(2):
            mid_copy(target).wait_send()

    for index in range(2):
        for copy in out_copies(index):
            copy.wait()


def shards(sources, initial_state, roughness, region_ids, diffusion_table, velocity_table):
    vmem, sems = pltpu.VMEM, pltpu.SemaphoreType.DMA
    scratch = dict(
        raw=vmem((4, 4, 256, 128), F32),
        maps=vmem((48, 512), F32),
        ids_wide=vmem((16, 128), jnp.int32),
        coef0=vmem((5, 32, 8, 512), F32),
        coef1=vmem((5, 16, 8, 256), F32),
        coef2=vmem((5, 8, 8, 128), F32),
        down1=vmem((512, 256), BF16),
        down2=vmem((256, 128), BF16),
        up1=vmem((128, 256), BF16),
        up0=vmem((256, 512), BF16),
        rhs=vmem((2, 34, 8, 512), F32),
        y=vmem((34, 8, 512), F32),
        work=vmem((2, 34, 8, 512), F32),
        tmid=vmem((32, 8, 512), F32),
        c_own=vmem((32, 8, 512), F32),
        y_in=vmem((34, 8, 512), F32),
        c_in=vmem((32, 8, 512), F32),
        third=vmem((32, 8, 512), F32),
        beta=vmem((16, 8, 256), F32),
        beta_in=vmem((8, 16, 8, 256), F32),
        mid_own=vmem((16, 8, 256), F32),
        mid_in=vmem((16, 8, 256), F32),
        level1=vmem((2, 18, 8, 256), F32),
        e_own=vmem((8, 8, 128), F32),
        e_in=vmem((8, 8, 8, 128), F32),
        g_own=vmem((8, 8, 128), F32),
        g_in=vmem((16, 8, 8, 128), F32),
        out_raw=vmem((2, 4, 256, 128), F32),
        in_sem=sems((4, 4)),
        out_sem=sems((2, 4)),
        y_send=sems((CHUNKS,)),
        y_recv=sems((CHUNKS,)),
        c_send=sems((2 * CHUNKS,)),
        c_recv=sems((CHUNKS,)),
        b_send=sems((3,)),
        b_recv=sems((8,)),
        m_send=sems((2,)),
        m_recv=sems(()),
        e_send=sems((8,)),
        e_recv=sems((8,)),
        g_send=sems((16,)),
        g_recv=sems((16,)),
    )
    anywhere = pl.BlockSpec(memory_space=pl.ANY)
    small = pl.BlockSpec(memory_space=pltpu.SMEM)
    return pl.pallas_call(
        kernel,
        out_shape=jax.ShapeDtypeStruct(sources.shape, F32),
        in_specs=[anywhere, anywhere, anywhere, pl.BlockSpec(memory_space=pltpu.VMEM), small, small],
        out_specs=anywhere,
        scratch_shapes=list(scratch.values()),
        compiler_params=pltpu.CompilerParams(
            collective_id=0, has_side_effects=True, vmem_limit_bytes=48 * 1024 * 1024
        ),
    )(sources, initial_state, roughness, region_ids, diffusion_table, velocity_table)


def solution(mesh):
    in_specs = (P(("tb", "ti"), None, None), P(), P(), P(), P(), P())
    out_specs = P(("tb", "ti"), None, None)
    return jax.shard_map(shards, mesh=mesh, in_specs=in_specs, out_specs=out_specs, check_vma=False)
```

time: 465 us -> 57.6 us (0.12)
  the two profiles are of different devices: /device:TPU:64 before, /device:TPU:67 now
where the time goes in v1:
time: 57.6 us; the launch traced here: 57.3 us
  Pallas kernels  52.2 us (91%)
  local copies, waits for them, and re-layouts  5.07 us (9%)
    pallas_call x1, Pallas kernels, shards(): pl.pallas_call(kernel, out_shape=jax.ShapeDtypeStruct(sources.shape, F32)...  52.2 us
    unnamed x12, local copies, waits for them, and re-layouts  5.07 us

profile of v1, /device:TPU:67, one launch (start us, length us, event | category | flops | bytes accessed | tf_op | source)
XLA Modules:
  0.0 57.3 jit_solution(1519114623266440720)
XLA Ops:
  0.0 0.0 copy-start.4
  0.0 0.0 copy-start.3
  0.0 0.8 %copy.7.velocity_table = f32[16,2]{1,0:T(8,128)S(1)} copy(f32[16,2]{0,1:T(2,128)} %param.11) | data formatting | bytes 256 | tf_op args[5]
  0.8 0.0 copy-done.4
  0.8 0.0 copy-done.3
  0.8 0.0 copy-start
  0.8 1.2 %copy-done = f32[2,256,512]{2,1,0:T(8,128)S(1)} copy-done((f32[2,256,512]{2,1,0:T(8,128)S(1)}, f32[2,256,512]{2,1,0:T(8,128)}, u32[]{:S(2)}) %copy-start) | copy-done | bytes 1048600
  2.0 0.0 copy-start.1
  2.0 1.0 %copy-done.1 = f32[256,512]{1,0:T(8,128)S(1)} copy-done((f32[256,512]{1,0:T(8,128)S(1)}, f32[256,512]{1,0:T(8,128)}, u32[]{:S(2)}) %copy-start.1) | copy-done | bytes 524312
  3.1 0.0 copy-start.2
  3.1 1.0 %copy-done.2 = f32[256,512]{1,0:T(8,128)S(1)} copy-done((f32[256,512]{1,0:T(8,128)S(1)}, f32[256,512]{1,0:T(8,128)}, u32[]{:S(2)}) %copy-start.2) | copy-done | bytes 524312
  4.1 52.2 %shard_map.64 = f32[2,256,512]{2,1,0:T(8,128)S(1)} custom-call(f32[2,256,512]{2,1,0:T(8,128)S(1)} %copy-done, f32[256,512]{1,0:T(8,128)S(1)} %copy-done.1, f32[256,512]{1,0:T(8,128)S(1)} %copy-done.2, s32[16,16]{1,0:T(8,128)S(1)} %copy-done.3, f32[16]{0:T(128)S(1)} %copy-done.4, f32[16,2]{1,0:T(8,128)S(1)} %copy.7.velocity_table), custom_call_target="tpu_custom_call" | custom-call | tf_op jit(solution)/shard_map/pallas_call | solution.py:587
  56.4 1.0 %copy.9 = f32[2,256,512]{2,1,0:T(8,128)} copy(f32[2,256,512]{2,1,0:T(8,128)S(1)} %shard_map.64) | data formatting | bytes 2097152
Async XLA Ops:
  0.0 0.8 %copy-start.4 = (f32[16]{0:T(128)S(1)}, f32[16]{0:T(128)}, u32[]{:S(2)}) copy-start(f32[16]{0:T(128)} %diffusion_table.1) | copy-start | bytes 196
  0.0 0.8 %copy-start.3 = (s32[16,16]{1,0:T(8,128)S(1)}, s32[16,16]{1,0:T(8,128)}, u32[]{:S(2)}) copy-start(s32[16,16]{1,0:T(8,128)} %ids.1) | copy-start | bytes 3076
  0.8 1.2 %copy-start = (f32[2,256,512]{2,1,0:T(8,128)S(1)}, f32[2,256,512]{2,1,0:T(8,128)}, u32[]{:S(2)}) copy-start(f32[2,256,512]{2,1,0:T(8,128)} %src.1) | copy-start | bytes 3145732
  2.0 1.0 %copy-start.1 = (f32[256,512]{1,0:T(8,128)S(1)}, f32[256,512]{1,0:T(8,128)}, u32[]{:S(2)}) copy-start(f32[256,512]{1,0:T(8,128)} %start.1) | copy-start | bytes 1572868
  3.1 1.0 %copy-start.2 = (f32[256,512]{1,0:T(8,128)S(1)}, f32[256,512]{1,0:T(8,128)}, u32[]{:S(2)}) copy-start(f32[256,512]{1,0:T(8,128)} %rough.1) | copy-start | bytes 1572868

commit v2 on v1

v2 whole, which is shorter than its diff:
```python
import functools

import jax
import jax.numpy as jnp
from jax import lax
from jax.experimental import pallas as pl
from jax.experimental.pallas import tpu as pltpu
from jax.sharding import PartitionSpec as P

MESH = pl.DeviceIdType.MESH
F32 = jnp.float32
BF16 = jnp.bfloat16

Y_CUTS = (0, 4, 8, 12, 16, 20, 24, 28, 32)
PIECES = len(Y_CUTS) - 1
C_PIECES = ((2, 6), (6, 10), (10, 14), (14, 18), (18, 22), (22, 26), (26, 32), (0, 2))
C_AFTER = (1, 2, 3, 4, 5, 6, 7, 7)
E_AFTER = 2


def wrap(ref, rows):
    ref[0] = pltpu.roll(ref[rows], 1, 0)
    ref[rows + 1] = pltpu.roll(ref[1], 7, 0)


def stencil(coef, r, centre, west, east):
    width = centre.shape[-1]
    south = pltpu.roll(centre, 1, 1)
    north = pltpu.roll(centre, width - 1, 1)
    return (
        (coef[0, r] * centre + coef[1, r] * west)
        + coef[2, r] * east
        + (coef[3, r] * south + coef[4, r] * north)
    )


def propagate(src, coef, rows, emit):
    wrap(src, rows)
    for r in range(rows):
        emit(r, stencil(coef, r, src[r + 1], src[r], src[r + 2]))


def into(dst):
    def emit(r, value):
        dst[r + 1] = value

    return emit


def exact_dot(x, matrix):
    first = x.astype(BF16)
    rest = x - first.astype(F32)
    second = rest.astype(BF16)
    third = (rest - second.astype(F32)).astype(BF16)

    def dot(part):
        return jnp.dot(part, matrix, preferred_element_type=F32)

    return dot(first) + (dot(second) + dot(third))


def pair_rows(value):
    rows, eight, width = value.shape
    halves = value.reshape(rows // 2, 2, eight, width)
    return halves[:, 0] + halves[:, 1]


def coarsen(value, matrix):
    rows, eight, width = value.shape
    summed = pair_rows(value).reshape(rows // 2 * eight, width)
    return exact_dot(summed, matrix).reshape(rows // 2, eight, width // 2)


def refine_lanes(value, matrix):
    rows, eight, width = value.shape
    return exact_dot(value.reshape(rows * eight, width), matrix).reshape(rows, eight, width * 2)


def put_refined(dst, value, matrix):
    wide = refine_lanes(value, matrix)
    for r in range(value.shape[0]):
        dst[2 * r + 1] = wide[r]
        dst[2 * r + 2] = wide[r]


def set_coefficients(coef, r, diffusion, speed_x, speed_y):
    coef[0, r] = 1.0 - 4.0 * diffusion - jnp.abs(speed_x) - jnp.abs(speed_y)
    coef[1, r] = diffusion + jnp.maximum(speed_x, 0.0)
    coef[2, r] = diffusion - jnp.minimum(speed_x, 0.0)
    coef[3, r] = diffusion + jnp.maximum(speed_y, 0.0)
    coef[4, r] = diffusion - jnp.minimum(speed_y, 0.0)


def block_matrix(rows, columns, wide_rows, entry):
    row = lax.broadcasted_iota(jnp.int32, (rows, columns), 0)
    column = lax.broadcasted_iota(jnp.int32, (rows, columns), 1)
    same = (row // 2 == column) if wide_rows else (row == column // 2)
    return jnp.where(same, entry, 0.0).astype(BF16)


def kernel(
    src, start, rough, ids, diffusion_table, velocity_table, out,
    raw, ids_raw, diffusion_entries, velocity_entries, maps, ids_wide, coef0, coef1, coef2, down1, down2, up1, up0,
    rhs, y, work, tmid, c_own, y_in, c_in, third, beta, swap_in, b_own, b_in, mid, mid_own, level1, e_own, e_in, g_own, g_in,
    out_raw, in_sem, small_sem, out_sem, y_send, y_recv, c_send, c_recv, s_send, s_recv, b_send, b_recv,
    e_send, e_recv, g_send, g_recv,
):
    tb, ti = lax.axis_index("tb"), lax.axis_index("ti")
    outer = lax.axis_size("tb")
    parity = lax.rem(ti, 2)
    odd = parity == 1
    even = parity == 0
    slot = ti // 2
    first_interval = (tb == 0) & (slot == 0)
    last_interval = (tb == outer - 1) & (slot == 3)
    next_tb = lax.rem(tb + jnp.where(slot == 3, 1, 0), outer)
    next_even = lax.rem(ti - parity + 2, 8)
    next_slot = lax.rem(slot + 1, 4)
    partner = ti + 1 - 2 * parity

    def load(index, array, part):
        return [
            pltpu.make_async_copy(
                array.at[:, pl.ds(128 * t, 128)] if part is None else array.at[part, :, pl.ds(128 * t, 128)],
                raw.at[index, t],
                in_sem.at[index, t],
            )
            for t in range(4)
        ]

    small = [
        pltpu.make_async_copy(ids, ids_raw, small_sem.at[0]),
        pltpu.make_async_copy(diffusion_table, diffusion_entries, small_sem.at[1]),
        pltpu.make_async_copy(velocity_table, velocity_entries, small_sem.at[2]),
    ]
    load_rough, load_first, load_second, load_start = load(0, rough, None), load(1, src, 0), load(2, src, 1), load(3, start, None)
    for copy in small + load_rough + load_first + load_second:
        copy.start()

    @pl.when(first_interval | last_interval)
    def _():
        for copy in load_start:
            copy.start()

    barrier = pltpu.get_barrier_semaphore()
    for d in range(1, 16):

        @pl.when(tb - d >= 0)
        def _():
            pl.semaphore_signal(barrier, 1, device_id=(tb - d, ti), device_id_type=MESH)

    for d in range(8):
        from_tb = lax.rem(tb + (outer - 1 if d >= 6 else 0), outer)

        @pl.when((from_tb != tb) | (ti != d))
        def _():
            pl.semaphore_signal(barrier, 1, device_id=(from_tb, d), device_id_type=MESH)

    @pl.when(ti >= 6)
    def _():
        pl.semaphore_signal(barrier, 1, device_id=(tb, partner), device_id_type=MESH)

    def raw_row(index, r):
        return jnp.concatenate([raw[index, t, pl.ds(r, 8, stride=32), :] for t in range(4)], axis=1)

    down1[...] = block_matrix(512, 256, True, 0.25)
    down2[...] = block_matrix(256, 128, True, 0.25)
    up1[...] = block_matrix(128, 256, False, 1.0)
    up0[...] = block_matrix(256, 512, False, 1.0)

    for copy in small:
        copy.wait()
    ids_wide[...] = jnp.full(ids_wide.shape, -1, jnp.int32)
    ids_wide[:, 0:16] = ids_raw[...]
    kinds = jnp.concatenate([ids_wide[pl.ds(h, 8, stride=2), :] for h in range(2)], axis=0)
    tables = [jnp.zeros(kinds.shape, F32) for _ in range(3)]
    for kind in range(16):
        hit = kinds == kind
        entries = (diffusion_entries[kind], velocity_entries[0, kind], velocity_entries[1, kind])
        for which in range(3):
            tables[which] = jnp.where(hit, entries[which], tables[which])

    def spread(cells, scale):
        column = lax.broadcasted_iota(jnp.int32, (128, 16 * cells), 0)
        cell = lax.broadcasted_iota(jnp.int32, (128, 16 * cells), 1)
        return jnp.where(cell // cells == column, scale, 0.0).astype(F32)

    stacked = jnp.concatenate(tables, axis=0)

    def expand(rows, cells, scale):
        return jnp.dot(rows, spread(cells, scale), precision=lax.Precision.HIGHEST, preferred_element_type=F32)

    maps[...] = expand(stacked, 32, 1.0)
    speeds1 = expand(stacked[16:], 16, 2.0)
    speeds2 = expand(stacked[16:], 8, 4.0)

    for copy in load_rough:
        copy.wait()
    for r in range(32):
        h = r // 16
        diffusion = maps[8 * h : 8 * h + 8] * raw_row(0, r)
        tmid[r] = diffusion
        set_coefficients(coef0, r, diffusion, maps[16 + 8 * h : 24 + 8 * h], maps[32 + 8 * h : 40 + 8 * h])

    for copy in load_first + load_second:
        copy.wait()
    for r in range(32):
        rhs[0, r + 1] = raw_row(1, r)
        rhs[1, r + 1] = raw_row(2, r)

    def add_second(r, value):
        total = value + rhs[1, r + 1]
        y[r + 1] = total
        work[0, r + 1] = total

    propagate(rhs.at[0], coef0, 32, add_second)

    @pl.when(first_interval | last_interval)
    def _():
        for copy in load_start:
            copy.wait()

    @pl.when(first_interval)
    def _():
        for r in range(32):
            c_in[r] = raw_row(3, r)

    @pl.when(last_interval)
    def _():
        for r in range(32):
            work[0, r + 1] = jnp.where(odd, raw_row(3, r), 0.0)

    def turn(i, carry):
        propagate(work.at[lax.rem(i, 2)], coef0, 32, into(work.at[1 - lax.rem(i, 2)]))
        return carry

    lax.fori_loop(0, jnp.where(odd, 4, 6), turn, 0)
    beta[...] = coarsen(work[0, 1:33], down1[...])

    diffusion1 = coarsen(tmid[...], down1[...])
    for r in range(16):
        h = r // 8
        set_coefficients(coef1, r, diffusion1[r], speeds1[8 * h : 8 * h + 8], speeds1[16 + 8 * h : 24 + 8 * h])
    diffusion2 = coarsen(diffusion1, down2[...])
    for r in range(8):
        h = r // 4
        set_coefficients(coef2, r, diffusion2[r], speeds2[8 * h : 8 * h + 8], speeds2[16 + 8 * h : 24 + 8 * h])

    def level1_turn(i, carry):
        propagate(level1.at[lax.rem(i, 2)], coef1, 16, into(level1.at[1 - lax.rem(i, 2)]))
        return carry

    level1[0, 1:17] = beta[...]
    count = 3 - next_slot
    lax.fori_loop(0, count, level1_turn, 0)
    e_own[...] = coarsen(level1[lax.rem(count, 2), 1:17], down2[...])

    pl.semaphore_wait(barrier, jnp.where(ti < 6, 7, 9) + outer - 1 - tb)

    def e_copy(target):
        return pltpu.make_async_remote_copy(
            src_ref=e_own,
            dst_ref=e_in.at[ti],
            send_sem=e_send.at[target],
            recv_sem=e_recv.at[ti],
            device_id=(next_tb, target),
            device_id_type=MESH,
        )

    for target in range(8):

        @pl.when((ti != target) | (next_tb != tb))
        def _():
            e_copy(target).start()

        @pl.when((ti == target) & (next_tb == tb))
        def _():
            e_in[target] = e_own[...]

    swap = pltpu.make_async_remote_copy(
        src_ref=beta.at[pl.ds(8 - 8 * parity, 8)],
        dst_ref=swap_in,
        send_sem=s_send,
        recv_sem=s_recv,
        device_id=(tb, partner),
        device_id_type=MESH,
    )
    swap.start()

    def y_copy(piece):
        low, high = Y_CUTS[piece], Y_CUTS[piece + 1]
        return pltpu.make_async_remote_copy(
            src_ref=y.at[pl.ds(1 + low, high - low)],
            dst_ref=y_in.at[pl.ds(1 + low, high - low)],
            send_sem=y_send.at[piece],
            recv_sem=y_recv.at[piece],
            device_id=(tb, partner),
            device_id_type=MESH,
        )

    @pl.when(even)
    def _():
        for piece in range(PIECES):
            y_copy(piece).start()

    def b_copy(target):
        return pltpu.make_async_remote_copy(
            src_ref=b_own,
            dst_ref=b_in.at[next_slot, pl.ds(8 * parity, 8)],
            send_sem=b_send.at[target],
            recv_sem=b_recv.at[2 * next_slot + parity],
            device_id=(next_tb, target),
            device_id_type=MESH,
        )

    def b_arrival(which, half):
        return pltpu.make_async_remote_copy(
            src_ref=b_own,
            dst_ref=b_in.at[which, pl.ds(8 * half, 8)],
            send_sem=b_send.at[0],
            recv_sem=b_recv.at[2 * which + half],
            device_id=(tb, partner),
            device_id_type=MESH,
        )

    swap.wait_recv()
    b_own[...] = beta[pl.ds(8 * parity, 8)] + swap_in[...]
    for target in range(1, 8):

        @pl.when((next_slot < 3) & (target >= 2 * next_slot + 1))
        def _():
            b_copy(target).start()

    def c_copy(piece, target):
        low, high = C_PIECES[piece]
        return pltpu.make_async_remote_copy(
            src_ref=c_own.at[pl.ds(low, high - low)],
            dst_ref=c_in.at[pl.ds(low, high - low)],
            send_sem=c_send.at[2 * piece + target],
            recv_sem=c_recv.at[piece],
            device_id=(next_tb, next_even + target),
            device_id_type=MESH,
        )

    def first_step(r):
        value = stencil(coef0, r, y_in[r + 1], y_in[r], y_in[r + 2])
        work[0, r + 1] = value
        third[r] = value + rhs[0, r + 1]

    def second_step(r):
        c_own[r] = stencil(coef0, r, work[0, r + 1], work[0, r], work[0, r + 2]) + y[r + 1]

    def end_state(piece):
        y_copy(piece).wait_recv()
        low, high = Y_CUTS[piece], Y_CUTS[piece + 1]
        if piece == PIECES - 1:
            wrap(y_in, 32)
        for r in range(max(low - 1, 1), 32 if high == 32 else high - 1):
            first_step(r)
        if high == 32:
            first_step(0)
            wrap(work.at[0], 32)
        for which, (begin, end) in enumerate(C_PIECES):
            if C_AFTER[which] != piece:
                continue
            for r in range(begin, end):
                second_step(r)

            @pl.when(jnp.logical_not(last_interval))
            def _():
                for target in (1, 0):
                    c_copy(which, target).start()

    @pl.when(odd)
    def _():
        for piece in range(E_AFTER):
            end_state(piece)

    def e_arrival(source):
        return pltpu.make_async_remote_copy(
            src_ref=e_own,
            dst_ref=e_in.at[source],
            send_sem=e_send.at[source],
            recv_sem=e_recv.at[source],
            device_id=(tb, source),
            device_id_type=MESH,
        )

    for source in range(8):

        @pl.when((ti != source) | (source >= 6))
        def _():
            e_arrival(source).wait_recv()

    total = e_in[0]
    for source in range(1, 8):
        total = total + e_in[source]
    g_own[...] = total

    def g_copy(d):
        return pltpu.make_async_remote_copy(
            src_ref=g_own,
            dst_ref=g_in.at[tb],
            send_sem=g_send.at[d],
            recv_sem=g_recv.at[tb],
            device_id=(tb + d, ti),
            device_id_type=MESH,
        )

    for d in range(1, 16):

        @pl.when(tb + d < outer)
        def _():
            g_copy(d).start()

    @pl.when(odd)
    def _():
        for piece in range(E_AFTER, PIECES):
            end_state(piece)

    def mid_turn(i, carry):
        for half in range(2):
            b_arrival(i, half).wait_recv()

        def emit(r, value):
            level1[1 - lax.rem(i, 2), r + 1] = value + b_in[i, r]

        propagate(level1.at[lax.rem(i, 2)], coef1, 16, emit)
        return carry

    level1[0] = jnp.zeros(level1.shape[1:], F32)
    lax.fori_loop(0, slot, mid_turn, 0)
    mid[...] = level1[lax.rem(slot, 2), 1:17]

    @pl.when(odd & (slot < 3))
    def _():
        mid_turn(slot, 0)
        mid_own[...] = level1[1 - lax.rem(slot, 2), 1:17]

    def level2(value):
        first = pltpu.roll(value[7], 1, 0)
        last = pltpu.roll(value[0], 7, 0)
        rows = [first] + [value[r] for r in range(8)] + [last]
        return jnp.stack([stencil(coef2, r, rows[r + 1], rows[r], rows[r + 2]) for r in range(8)])

    def g_arrival(source):
        return pltpu.make_async_remote_copy(
            src_ref=g_own,
            dst_ref=g_in.at[source],
            send_sem=g_send.at[0],
            recv_sem=g_recv.at[source],
            device_id=(0, ti),
            device_id_type=MESH,
        )

    def chain_turn(source, state):
        g_arrival(source).wait_recv()
        return level2(state) + g_in[source]

    before = lax.fori_loop(0, tb, chain_turn, jnp.zeros((8, 8, 128), F32))
    g_in[tb] = level2(before) + g_own[...]

    put_refined(level1.at[0], before, up1[...])
    lax.fori_loop(0, slot, level1_turn, 0)
    here = lax.rem(slot, 2)
    wide = refine_lanes(level1[here, 1:17] + mid[...], up0[...])

    @pl.when(jnp.logical_not(first_interval))
    def _():
        for piece in range(len(C_PIECES)):
            c_copy(piece, 0).wait_recv()

    for r in range(32):
        work[0, r + 1] = c_in[r] + wide[r // 2]

    def put_out(index, r, value):
        for t in range(4):
            out_raw[index, t, pl.ds(r, 8, stride=32), :] = value[:, 128 * t : 128 * t + 128]

    def out_copies(index):
        return [
            pltpu.make_async_copy(out_raw.at[index, t], out.at[index, :, pl.ds(128 * t, 128)], out_sem.at[index, t])
            for t in range(4)
        ]

    @pl.when(even)
    def _():
        def emit_first(r, value):
            state = value + rhs[0, r + 1]
            work[1, r + 1] = state
            put_out(0, r, state)

        propagate(work.at[0], coef0, 32, emit_first)
        for copy in out_copies(0):
            copy.start()

        def emit_second(r, value):
            put_out(1, r, value + rhs[1, r + 1])

        propagate(work.at[1], coef0, 32, emit_second)

    @pl.when(odd)
    def _():
        @pl.when(slot < 3)
        def _():
            def emit_end(r, value):
                mid_own[r] = value + mid_own[r]

            propagate(level1.at[here], coef1, 16, emit_end)

        @pl.when(slot == 3)
        def _():
            fixed = refine_lanes(g_in[tb], up1[...])
            for r in range(16):
                mid_own[r] = fixed[r // 2]

        wide = refine_lanes(mid_own[...], up0[...])
        for r in range(32):
            put_out(1, r, c_own[r] + wide[r // 2])
        for copy in out_copies(1):
            copy.start()
        propagate(work.at[0], coef0, 32, into(work.at[1]))
        propagate(work.at[1], coef0, 32, into(work.at[0]))

        def emit(r, value):
            put_out(0, r, value + third[r])

        propagate(work.at[0], coef0, 32, emit)
        for copy in out_copies(0):
            copy.start()

    @pl.when(even)
    def _():
        for copy in out_copies(1):
            copy.start()

    swap.wait_send()

    @pl.when(even)
    def _():
        for piece in range(PIECES):
            y_copy(piece).wait_send()

    for target in range(1, 8):

        @pl.when((next_slot < 3) & (target >= 2 * next_slot + 1))
        def _():
            b_copy(target).wait_send()

    for target in range(8):

        @pl.when((ti != target) | (next_tb != tb))
        def _():
            e_copy(target).wait_send()

    for d in range(1, 16):

        @pl.when(tb + d < outer)
        def _():
            g_copy(d).wait_send()

    @pl.when(odd & jnp.logical_not(last_interval))
    def _():
        for piece in range(len(C_PIECES)):
            for target in range(2):
                c_copy(piece, target).wait_send()

    for index in range(2):
        for copy in out_copies(index):
            copy.wait()


def shards(sources, initial_state, roughness, region_ids, diffusion_table, velocity_table):
    vmem, sems = pltpu.VMEM, pltpu.SemaphoreType.DMA
    scratch = dict(
        raw=vmem((4, 4, 256, 128), F32),
        ids_raw=vmem((16, 16), jnp.int32),
        diffusion_entries=pltpu.SMEM((16,), F32),
        velocity_entries=pltpu.SMEM((2, 16), F32),
        maps=vmem((48, 512), F32),
        ids_wide=vmem((16, 128), jnp.int32),
        coef0=vmem((5, 32, 8, 512), F32),
        coef1=vmem((5, 16, 8, 256), F32),
        coef2=vmem((5, 8, 8, 128), F32),
        down1=vmem((512, 256), BF16),
        down2=vmem((256, 128), BF16),
        up1=vmem((128, 256), BF16),
        up0=vmem((256, 512), BF16),
        rhs=vmem((2, 34, 8, 512), F32),
        y=vmem((34, 8, 512), F32),
        work=vmem((2, 34, 8, 512), F32),
        tmid=vmem((32, 8, 512), F32),
        c_own=vmem((32, 8, 512), F32),
        y_in=vmem((34, 8, 512), F32),
        c_in=vmem((32, 8, 512), F32),
        third=vmem((32, 8, 512), F32),
        beta=vmem((16, 8, 256), F32),
        swap_in=vmem((8, 8, 256), F32),
        b_own=vmem((8, 8, 256), F32),
        b_in=vmem((3, 16, 8, 256), F32),
        mid=vmem((16, 8, 256), F32),
        mid_own=vmem((16, 8, 256), F32),
        level1=vmem((2, 18, 8, 256), F32),
        e_own=vmem((8, 8, 128), F32),
        e_in=vmem((8, 8, 8, 128), F32),
        g_own=vmem((8, 8, 128), F32),
        g_in=vmem((16, 8, 8, 128), F32),
        out_raw=vmem((2, 4, 256, 128), F32),
        in_sem=sems((4, 4)),
        small_sem=sems((3,)),
        out_sem=sems((2, 4)),
        y_send=sems((PIECES,)),
        y_recv=sems((PIECES,)),
        c_send=sems((2 * len(C_PIECES),)),
        c_recv=sems((len(C_PIECES),)),
        s_send=sems(()),
        s_recv=sems(()),
        b_send=sems((8,)),
        b_recv=sems((6,)),
        e_send=sems((8,)),
        e_recv=sems((8,)),
        g_send=sems((16,)),
        g_recv=sems((16,)),
    )
    anywhere = pl.BlockSpec(memory_space=pl.ANY)
    return pl.pallas_call(
        kernel,
        out_shape=pltpu.VMEM(sources.shape, F32),
        in_specs=[pl.BlockSpec(memory_space=pltpu.HBM)] * 6,
        out_specs=anywhere,
        scratch_shapes=list(scratch.values()),
        compiler_params=pltpu.CompilerParams(
            collective_id=0, has_side_effects=True, vmem_limit_bytes=60 * 1024 * 1024
        ),
    )(sources, initial_state, roughness, region_ids, diffusion_table, velocity_table.T)


def solution(mesh):
    in_specs = (P(("tb", "ti"), None, None), P(), P(), P(), P(), P())
    out_specs = P(("tb", "ti"), None, None)
    return jax.shard_map(shards, mesh=mesh, in_specs=in_specs, out_specs=out_specs, check_vma=False)
```

time: 57.6 us -> 41.5 us (0.72)
  Pallas kernels: 52.2 us -> 40.4 us
  local copies, waits for them, and re-layouts: 5.07 us -> 0.97 us
    pallas_call x1, Pallas kernels: 52.2 us -> 40.4 us  [shards(): pl.pallas_call(kernel, out_shape=pltpu.VMEM(sources.shape, F32), in_specs...]
    unnamed x12 -> x1, local copies, waits for them, and re-layouts: 5.07 us -> 0.97 us
where the time goes in v2:
time: 41.5 us; the launch traced here: 41.4 us
  Pallas kernels  40.4 us (97%)
  local copies, waits for them, and re-layouts  0.97 us (2%)
    pallas_call x1, Pallas kernels, shards(): pl.pallas_call(kernel, out_shape=pltpu.VMEM(sources.shape, F32), in_specs...  40.4 us
    unnamed x1, local copies, waits for them, and re-layouts  0.97 us

profile of v2, /device:TPU:67, one launch (start us, length us, event | category | flops | bytes accessed | tf_op | source)
XLA Modules:
  0.0 41.4 jit_solution(1494584953933616363)
XLA Ops:
  0.0 40.4 %shard_map.64 = f32[2,256,512]{2,1,0:T(8,128)S(1)} custom-call(f32[2,256,512]{2,1,0:T(8,128)} %src.1, f32[256,512]{1,0:T(8,128)} %start.1, f32[256,512]{1,0:T(8,128)} %rough.1, s32[16,16]{1,0:T(8,128)} %ids.1, f32[16]{0:T(128)} %diffusion_table.1, f32[2,16]{1,0:T(2,128)} %bitcast.1), custom_call_target="tpu_custom_call" | custom-call | tf_op jit(solution)/shard_map/pallas_call | solution.py:626
  40.4 1.0 %copy.8 = f32[2,256,512]{2,1,0:T(8,128)} copy(f32[2,256,512]{2,1,0:T(8,128)S(1)} %shard_map.64) | data formatting | bytes 2097152

commit v3 on v2

--- a/solution.py
+++ b/solution.py
@@ -16,6 +16,8 @@
 C_PIECES = ((2, 6), (6, 10), (10, 14), (14, 18), (18, 22), (22, 26), (26, 32), (0, 2))
 C_AFTER = (1, 2, 3, 4, 5, 6, 7, 7)
 E_AFTER = 2
+EARLY_TURNS = 1
+Y_EARLY = 2
 
 
 def wrap(ref, rows):
@@ -103,7 +105,8 @@
     raw, ids_raw, diffusion_entries, velocity_entries, maps, ids_wide, coef0, coef1, coef2, down1, down2, up1, up0,
     rhs, y, work, tmid, c_own, y_in, c_in, third, beta, swap_in, b_own, b_in, mid, mid_own, level1, e_own, e_in, g_own, g_in,
     out_raw, in_sem, small_sem, out_sem, y_send, y_recv, c_send, c_recv, s_send, s_recv, b_send, b_recv,
-    e_send, e_recv, g_send, g_recv,
+    e_send, e_recv, g_send, g_recv, start_beta, start_e, start_e_send, start_b_send, ready_far, ready_all,
+    states, w_send, w_recv,
 ):
     tb, ti = lax.axis_index("tb"), lax.axis_index("ti")
     outer = lax.axis_size("tb")
@@ -113,6 +116,8 @@
     slot = ti // 2
     first_interval = (tb == 0) & (slot == 0)
     last_interval = (tb == outer - 1) & (slot == 3)
+    has_next = jnp.logical_not(last_interval)
+    start_share = (tb == 0) & (slot == 3)
     next_tb = lax.rem(tb + jnp.where(slot == 3, 1, 0), outer)
     next_even = lax.rem(ti - parity + 2, 8)
     next_slot = lax.rem(slot + 1, 4)
@@ -137,28 +142,31 @@
     for copy in small + load_rough + load_first + load_second:
         copy.start()
 
-    @pl.when(first_interval | last_interval)
+    @pl.when(first_interval | start_share)
     def _():
         for copy in load_start:
             copy.start()
 
     barrier = pltpu.get_barrier_semaphore()
-    for d in range(1, 16):
-
-        @pl.when(tb - d >= 0)
-        def _():
-            pl.semaphore_signal(barrier, 1, device_id=(tb - d, ti), device_id_type=MESH)
-
-    for d in range(8):
-        from_tb = lax.rem(tb + (outer - 1 if d >= 6 else 0), outer)
-
-        @pl.when((from_tb != tb) | (ti != d))
-        def _():
-            pl.semaphore_signal(barrier, 1, device_id=(from_tb, d), device_id_type=MESH)
-
-    @pl.when(ti >= 6)
-    def _():
-        pl.semaphore_signal(barrier, 1, device_id=(tb, partner), device_id_type=MESH)
+
+    def greet(to_tb, to_ti):
+        pl.semaphore_signal(barrier, 1, device_id=(to_tb, to_ti), device_id_type=MESH)
+
+    def across(bits):
+        return tb + sum((bit - 2 * bit * lax.rem(tb // bit, 2)) for bit in bits)
+
+    @pl.when(even)
+    def _():
+        for bits in ((1,), (2,), (4,), (2, 4), (8,)):
+            greet(across(bits), ti)
+
+    for d in range(1, 8):
+        greet(tb, lax.rem(ti + d, 8))
+
+    @pl.when(tb > 0)
+    def _():
+        for d in (6, 7):
+            greet(tb - 1, d)
 
     def raw_row(index, r):
         return jnp.concatenate([raw[index, t, pl.ds(r, 8, stride=32), :] for t in range(4)], axis=1)
@@ -215,28 +223,6 @@
 
     propagate(rhs.at[0], coef0, 32, add_second)
 
-    @pl.when(first_interval | last_interval)
-    def _():
-        for copy in load_start:
-            copy.wait()
-
-    @pl.when(first_interval)
-    def _():
-        for r in range(32):
-            c_in[r] = raw_row(3, r)
-
-    @pl.when(last_interval)
-    def _():
-        for r in range(32):
-            work[0, r + 1] = jnp.where(odd, raw_row(3, r), 0.0)
-
-    def turn(i, carry):
-        propagate(work.at[lax.rem(i, 2)], coef0, 32, into(work.at[1 - lax.rem(i, 2)]))
-        return carry
-
-    lax.fori_loop(0, jnp.where(odd, 4, 6), turn, 0)
-    beta[...] = coarsen(work[0, 1:33], down1[...])
-
     diffusion1 = coarsen(tmid[...], down1[...])
     for r in range(16):
         h = r // 8
@@ -246,16 +232,106 @@
         h = r // 4
         set_coefficients(coef2, r, diffusion2[r], speeds2[8 * h : 8 * h + 8], speeds2[16 + 8 * h : 24 + 8 * h])
 
+    def y_copy(piece):
+        low, high = Y_CUTS[piece], Y_CUTS[piece + 1]
+        return pltpu.make_async_remote_copy(
+            src_ref=y.at[pl.ds(1 + low, high - low)],
+            dst_ref=y_in.at[pl.ds(1 + low, high - low)],
+            send_sem=y_send.at[piece],
+            recv_sem=y_recv.at[piece],
+            device_id=(tb, partner),
+            device_id_type=MESH,
+        )
+
+    def turn(i, carry):
+        propagate(work.at[lax.rem(i, 2)], coef0, 32, into(work.at[1 - lax.rem(i, 2)]))
+        return carry
+
     def level1_turn(i, carry):
         propagate(level1.at[lax.rem(i, 2)], coef1, 16, into(level1.at[1 - lax.rem(i, 2)]))
         return carry
+
+    @pl.when(first_interval | start_share)
+    def _():
+        for copy in load_start:
+            copy.wait()
+
+    @pl.when(first_interval)
+    def _():
+        for r in range(32):
+            c_in[r] = raw_row(3, r)
+
+    @pl.when(start_share)
+    def _():
+        for r in range(32):
+            work[0, r + 1] = raw_row(3, r)
+        lax.fori_loop(0, 4, turn, 0)
+        start_beta[...] = coarsen(work[0, 1:33], down1[...])
+        level1[0, 1:17] = start_beta[...]
+        lax.fori_loop(0, 3, level1_turn, 0)
+        start_e[...] = coarsen(level1[1, 1:17], down2[...])
+        for r in range(32):
+            work[0, r + 1] = y[r + 1]
+
+    lax.fori_loop(0, EARLY_TURNS, turn, 0)
+
+    pl.semaphore_wait(barrier, 7 + jnp.where(even, 5, 0) + jnp.where((ti >= 6) & (tb < outer - 1), 8, 0))
+
+    @pl.when(even)
+    def _():
+        pl.semaphore_signal(ready_far, 1, device_id=(across((8,)), ti), device_id_type=MESH)
+
+
+    @pl.when(even)
+    def _():
+        for piece in range(Y_EARLY):
+            y_copy(piece).start()
+
+    def start_e_copy(target):
+        return pltpu.make_async_remote_copy(
+            src_ref=start_e,
+            dst_ref=e_in.at[7],
+            send_sem=start_e_send.at[target],
+            recv_sem=e_recv.at[7],
+            device_id=(tb, target),
+            device_id_type=MESH,
+        )
+
+    def start_b_copy(target):
+        return pltpu.make_async_remote_copy(
+            src_ref=start_beta.at[pl.ds(8 * parity, 8)],
+            dst_ref=b_in.at[0, pl.ds(8 * parity, 8)],
+            send_sem=start_b_send.at[target],
+            recv_sem=b_recv.at[parity],
+            device_id=(tb, target),
+            device_id_type=MESH,
+        )
+
+    @pl.when(start_share & odd)
+    def _():
+        for target in range(0, 8, 2):
+            start_e_copy(target).start()
+
+    @pl.when(start_share)
+    def _():
+        b_in[0, pl.ds(8 * parity, 8)] = start_beta[pl.ds(8 * parity, 8)]
+        for target in range(1, 8):
+
+            @pl.when(ti != target)
+            def _():
+                start_b_copy(target).start()
+
+    @pl.when(tb == 0)
+    def _():
+        e_in[6] = jnp.zeros(e_own.shape, F32)
+
+    lax.fori_loop(EARLY_TURNS, jnp.where(odd, 4, 6), turn, 0)
+    beta[...] = coarsen(work[0, 1:33], down1[...])
 
     level1[0, 1:17] = beta[...]
     count = 3 - next_slot
     lax.fori_loop(0, count, level1_turn, 0)
     e_own[...] = coarsen(level1[lax.rem(count, 2), 1:17], down2[...])
-
-    pl.semaphore_wait(barrier, jnp.where(ti < 6, 7, 9) + outer - 1 - tb)
 
     def e_copy(target):
         return pltpu.make_async_remote_copy(
@@ -267,13 +343,13 @@
             device_id_type=MESH,
         )
 
-    for target in range(8):
-
-        @pl.when((ti != target) | (next_tb != tb))
+    for target in range(0, 8, 2):
+
+        @pl.when(has_next & ((ti != target) | (slot == 3)))
         def _():
             e_copy(target).start()
 
-        @pl.when((ti == target) & (next_tb == tb))
+        @pl.when((ti == target) & (slot < 3))
         def _():
             e_in[target] = e_own[...]
 
@@ -287,22 +363,6 @@
     )
     swap.start()
 
-    def y_copy(piece):
-        low, high = Y_CUTS[piece], Y_CUTS[piece + 1]
-        return pltpu.make_async_remote_copy(
-            src_ref=y.at[pl.ds(1 + low, high - low)],
-            dst_ref=y_in.at[pl.ds(1 + low, high - low)],
-            send_sem=y_send.at[piece],
-            recv_sem=y_recv.at[piece],
-            device_id=(tb, partner),
-            device_id_type=MESH,
-        )
-
-    @pl.when(even)
-    def _():
-        for piece in range(PIECES):
-            y_copy(piece).start()
-
     def b_copy(target):
         return pltpu.make_async_remote_copy(
             src_ref=b_own,
@@ -323,11 +383,21 @@
             device_id_type=MESH,
         )
 
+    @pl.when(even)
+    def _():
+        for piece in range(Y_EARLY, PIECES):
+            y_copy(piece).start()
+
+    @pl.when(even)
+    def _():
+        pl.semaphore_wait(ready_far, 1)
+        pl.semaphore_signal(ready_all, 1, device_id=(across((1,)), ti), device_id_type=MESH)
+
     swap.wait_recv()
     b_own[...] = beta[pl.ds(8 * parity, 8)] + swap_in[...]
     for target in range(1, 8):
 
-        @pl.when((next_slot < 3) & (target >= 2 * next_slot + 1))
+        @pl.when(has_next & (next_slot < 3) & (target >= 2 * next_slot + 1))
         def _():
             b_copy(target).start()
 
@@ -386,17 +456,6 @@
             device_id_type=MESH,
         )
 
-    for source in range(8):
-
-        @pl.when((ti != source) | (source >= 6))
-        def _():
-            e_arrival(source).wait_recv()
-
-    total = e_in[0]
-    for source in range(1, 8):
-        total = total + e_in[source]
-    g_own[...] = total
-
     def g_copy(d):
         return pltpu.make_async_remote_copy(
             src_ref=g_own,
@@ -407,11 +466,25 @@
             device_id_type=MESH,
         )
 
-    for d in range(1, 16):
-
-        @pl.when(tb + d < outer)
-        def _():
-            g_copy(d).start()
+    @pl.when(even)
+    def _():
+        for source in range(8):
+
+            @pl.when((ti != source) if source < 6 else ((tb > 0) | (source == 7)))
+            def _():
+                e_arrival(source).wait_recv()
+
+        total = e_in[0]
+        for source in range(1, 8):
+            total = total + e_in[source]
+        g_own[...] = total
+
+        pl.semaphore_wait(ready_all, 1)
+        for d in range(1, 16):
+
+            @pl.when(tb + d < outer)
+            def _():
+                g_copy(d).start()
 
     @pl.when(odd)
     def _():
@@ -420,7 +493,10 @@
 
     def mid_turn(i, carry):
         for half in range(2):
-            b_arrival(i, half).wait_recv()
+
+            @pl.when((i > 0) | (tb > 0) | (ti != 6 + half))
+            def _():
+                b_arrival(i, half).wait_recv()
 
         def emit(r, value):
             level1[1 - lax.rem(i, 2), r + 1] = value + b_in[i, r]
@@ -457,21 +533,35 @@
         g_arrival(source).wait_recv()
         return level2(state) + g_in[source]
 
-    before = lax.fori_loop(0, tb, chain_turn, jnp.zeros((8, 8, 128), F32))
-    g_in[tb] = level2(before) + g_own[...]
-
-    put_refined(level1.at[0], before, up1[...])
+    def state_copy(which):
+        return pltpu.make_async_remote_copy(
+            src_ref=states.at[which],
+            dst_ref=states.at[which],
+            send_sem=w_send.at[which],
+            recv_sem=w_recv.at[which],
+            device_id=(tb, partner),
+            device_id_type=MESH,
+        )
+
+    @pl.when(even)
+    def _():
+        before = lax.fori_loop(0, tb, chain_turn, jnp.zeros((8, 8, 128), F32))
+        states[0] = before
+        state_copy(0).start()
+
+        @pl.when(slot == 3)
+        def _():
+            states[1] = level2(before) + g_own[...]
+            state_copy(1).start()
+
+    @pl.when(odd)
+    def _():
+        state_copy(0).wait_recv()
+
+    put_refined(level1.at[0], states[0], up1[...])
     lax.fori_loop(0, slot, level1_turn, 0)
     here = lax.rem(slot, 2)
     wide = refine_lanes(level1[here, 1:17] + mid[...], up0[...])
-
-    @pl.when(jnp.logical_not(first_interval))
-    def _():
-        for piece in range(len(C_PIECES)):
-            c_copy(piece, 0).wait_recv()
-
-    for r in range(32):
-        work[0, r + 1] = c_in[r] + wide[r // 2]
 
     def put_out(index, r, value):
         for t in range(4):
@@ -483,6 +573,36 @@
             for t in range(4)
         ]
 
+    @pl.when(odd)
+    def _():
+        @pl.when(slot < 3)
+        def _():
+            def emit_end(r, value):
+                mid_own[r] = value + mid_own[r]
+
+            propagate(level1.at[here], coef1, 16, emit_end)
+
+        @pl.when(slot == 3)
+        def _():
+            state_copy(1).wait_recv()
+            fixed = refine_lanes(states[1], up1[...])
+            for r in range(16):
+                mid_own[r] = fixed[r // 2]
+
+        wide_end = refine_lanes(mid_own[...], up0[...])
+        for r in range(32):
+            put_out(1, r, c_own[r] + wide_end[r // 2])
+        for copy in out_copies(1):
+            copy.start()
+
+    @pl.when(jnp.logical_not(first_interval))
+    def _():
+        for piece in range(len(C_PIECES)):
+            c_copy(piece, 0).wait_recv()
+
+    for r in range(32):
+        work[0, r + 1] = c_in[r] + wide[r // 2]
+
     @pl.when(even)
     def _():
         def emit_first(r, value):
@@ -501,24 +621,6 @@
 
     @pl.when(odd)
     def _():
-        @pl.when(slot < 3)
-        def _():
-            def emit_end(r, value):
-                mid_own[r] = value + mid_own[r]
-
-            propagate(level1.at[here], coef1, 16, emit_end)
-
-        @pl.when(slot == 3)
-        def _():
-            fixed = refine_lanes(g_in[tb], up1[...])
-            for r in range(16):
-                mid_own[r] = fixed[r // 2]
-
-        wide = refine_lanes(mid_own[...], up0[...])
-        for r in range(32):
-            put_out(1, r, c_own[r] + wide[r // 2])
-        for copy in out_copies(1):
-            copy.start()
         propagate(work.at[0], coef0, 32, into(work.at[1]))
         propagate(work.at[1], coef0, 32, into(work.at[0]))
 
@@ -543,21 +645,42 @@
 
     for target in range(1, 8):
 
-        @pl.when((next_slot < 3) & (target >= 2 * next_slot + 1))
+        @pl.when(has_next & (next_slot < 3) & (target >= 2 * next_slot + 1))
         def _():
             b_copy(target).wait_send()
 
-    for target in range(8):
-
-        @pl.when((ti != target) | (next_tb != tb))
+    for target in range(0, 8, 2):
+
+        @pl.when(has_next & ((ti != target) | (slot == 3)))
         def _():
             e_copy(target).wait_send()
 
+    @pl.when(start_share & odd)
+    def _():
+        for target in range(0, 8, 2):
+            start_e_copy(target).wait_send()
+
+    @pl.when(start_share)
+    def _():
+        for target in range(1, 8):
+
+            @pl.when(ti != target)
+            def _():
+                start_b_copy(target).wait_send()
+
     for d in range(1, 16):
 
-        @pl.when(tb + d < outer)
+        @pl.when(even & (tb + d < outer))
         def _():
             g_copy(d).wait_send()
+
+    @pl.when(even)
+    def _():
+        state_copy(0).wait_send()
+
+        @pl.when(slot == 3)
+        def _():
+            state_copy(1).wait_send()
 
     @pl.when(odd & jnp.logical_not(last_interval))
     def _():
@@ -621,6 +744,15 @@
         e_recv=sems((8,)),
         g_send=sems((16,)),
         g_recv=sems((16,)),
+        start_beta=vmem((16, 8, 256), F32),
+        start_e=vmem((8, 8, 128), F32),
+        start_e_send=sems((8,)),
+        start_b_send=sems((8,)),
+        ready_far=pltpu.SemaphoreType.REGULAR,
+        ready_all=pltpu.SemaphoreType.REGULAR,
+        states=vmem((2, 8, 8, 128), F32),
+        w_send=sems((2,)),
+        w_recv=sems((2,)),
     )
     anywhere = pl.BlockSpec(memory_space=pl.ANY)
     return pl.pallas_call(

time: 41.5 us -> 40.1 us (0.966)
  the two profiles are of different devices: /device:TPU:67 before, /device:TPU:114 now
where the time goes in v3:
time: 40.1 us; the launch traced here: 40 us
  Pallas kernels  39 us (97%)
  local copies, waits for them, and re-layouts  0.97 us (2%)
    pallas_call x1, Pallas kernels, shards(): pl.pallas_call(kernel, out_shape=pltpu.VMEM(sources.shape, F32), in_specs...  39 us
    unnamed x1, local copies, waits for them, and re-layouts  0.97 us

profile of v3, /device:TPU:114, one launch (start us, length us, event | category | flops | bytes accessed | tf_op | source)
XLA Modules:
  0.0 40.0 jit_solution(6740276261885618923)
XLA Ops:
  0.0 39.0 %shard_map.64 = f32[2,256,512]{2,1,0:T(8,128)S(1)} custom-call(f32[2,256,512]{2,1,0:T(8,128)} %src.1, f32[256,512]{1,0:T(8,128)} %start.1, f32[256,512]{1,0:T(8,128)} %rough.1, s32[16,16]{1,0:T(8,128)} %ids.1, f32[16]{0:T(128)} %diffusion_table.1, f32[2,16]{1,0:T(2,128)} %bitcast.1), custom_call_target="tpu_custom_call" | custom-call | tf_op jit(solution)/shard_map/pallas_call | solution.py:758
  39.0 1.0 %copy.8 = f32[2,256,512]{2,1,0:T(8,128)} copy(f32[2,256,512]{2,1,0:T(8,128)S(1)} %shard_map.64) | data formatting | bytes 2097152
